TPU v7x, 32 devices: a whole 2x2x4 slice. The times are simulated.
32 devices in a mesh: dp: 8 (over z, x), ctx: 4 (over y, core).
Axes of the slice: x: 2, y: 2, z: 4, core: 2. Of those that a mesh axis runs over, the one named last changes fastest.
Arguments:
- tokens_in: bfloat16 [16, 1024, 768], P('dp', 'ctx'), may hold values from -6 to 6
- out_grad: bfloat16 [16, 1024, 768], P('dp', 'ctx'), may hold values from -6 to 6
- w_query: bfloat16 [768, 768], P(('dp', 'ctx')), may hold values from -0.3125 to 0.3125
- w_key: bfloat16 [768, 768], P(('dp', 'ctx')), may hold values from -0.21875 to 0.21875
- w_value: bfloat16 [768, 768], P(('dp', 'ctx')), may hold values from -0.21875 to 0.21875
- w_out: bfloat16 [768, 768], P(('dp', 'ctx')), may hold values from -0.875 to 0.875
- w_up: bfloat16 [768, 3072], P(('dp', 'ctx')), may hold values from -0.21875 to 0.21875
- w_down: bfloat16 [3072, 768], P(('dp', 'ctx')), may hold values from -0.109375 to 0.109375
- b_query: bfloat16 [768], P(('dp', 'ctx')), may hold values from -4 to 4
- b_value: bfloat16 [768], P(('dp', 'ctx')), may hold values from -4 to 4
- b_out: bfloat16 [768], P(('dp', 'ctx')), may hold values from -4 to 4
- b_up: bfloat16 [3072], P(('dp', 'ctx')), may hold values from -4 to 4
- b_down: bfloat16 [768], P(('dp', 'ctx')), may hold values from -4 to 4
- norm1_gain: bfloat16 [768], P(('dp', 'ctx')), may hold values from 0.25 to 1.75
- norm1_shift: bfloat16 [768], P(('dp', 'ctx')), may hold values from -4 to 4
- norm2_gain: bfloat16 [768], P(('dp', 'ctx')), may hold values from 0.25 to 1.75
- norm2_shift: bfloat16 [768], P(('dp', 'ctx')), may hold values from -4 to 4
Outputs:
- layer_out: bfloat16 [16, 1024, 768], P('dp', 'ctx')
- grad_tokens: float32 [16, 1024, 768], P('dp', 'ctx')
- grad_w_query: float32 [768, 768], P(('dp', 'ctx'))
- grad_w_key: float32 [768, 768], P(('dp', 'ctx'))
- grad_w_value: float32 [768, 768], P(('dp', 'ctx'))
- grad_w_out: float32 [768, 768], P(('dp', 'ctx'))
- grad_w_up: float32 [768, 3072], P(('dp', 'ctx'))
- grad_w_down: float32 [3072, 768], P(('dp', 'ctx'))
- grad_b_query: float32 [768], P(('dp', 'ctx'))
- grad_b_value: float32 [768], P(('dp', 'ctx'))
- grad_b_out: float32 [768], P(('dp', 'ctx'))
- grad_b_up: float32 [3072], P(('dp', 'ctx'))
- grad_b_down: float32 [768], P(('dp', 'ctx'))
- grad_norm1_gain: float32 [768], P(('dp', 'ctx'))
- grad_norm1_shift: float32 [768], P(('dp', 'ctx'))
- grad_norm2_gain: float32 [768], P(('dp', 'ctx'))
- grad_norm2_shift: float32 [768], P(('dp', 'ctx'))
All inputs are finite; a program needn't handle non-finite values.
Results may differ from a plain program's by a relative error of at most 0.017.
Values may be sent and summed in bfloat16 or wider, within the bound.
No kernel may reach another device: no remote copies, remote signals or barrier semaphores. Data moves between devices by JAX's collectives and lax.ppermute only.
A program may use at most 192 MiB of HBM per device.

v0:
```python
import jax
import jax.numpy as jnp
from jax import lax
from jax.experimental import pallas as pl
from jax.experimental.pallas import tpu as pltpu
from jax.sharding import Mesh
from jax.sharding import PartitionSpec as P

HEADS = 12
DH = 64
MICRO = 2


def shifted(value, axis, by):
    peers = lax.axis_size(axis)
    return lax.ppermute(value, axis, [(i, (i + by) % peers) for i in range(peers)])


def as_sent(value):
    return jax.tree.map(lambda a: a.astype(jnp.bfloat16) if a.dtype == jnp.float32 else a, value)


def layer_norm(values, norm_gain, norm_shift):
    centre = values - jnp.mean(values, axis=-1, keepdims=True)
    spread = jnp.mean(centre * centre, axis=-1, keepdims=True)
    return centre * lax.rsqrt(spread + 1e-05) * norm_gain + norm_shift


def gelu_tanh(values):
    return (
        0.5
        * values
        * (1.0 + jnp.tanh(0.7978845608028654 * (values + 0.044715 * values * values * values)))
    )


def project(left, right):
    return jnp.einsum("scd,de->sce", left, right, preferred_element_type=jnp.float32)


def project_back(left, right):
    return jnp.einsum("sce,de->scd", left, right, preferred_element_type=jnp.float32)


def weight_grad(left, right):
    return jnp.einsum("scd,sce->de", left, right, preferred_element_type=jnp.float32)


def column_sum(values):
    return jnp.sum(values.astype(jnp.float32), axis=(0, 1))


def masked_scores(query_heads, key_full, first_pos):
    seq_count, key_len = (key_full.shape[0], key_full.shape[1])
    key_heads = key_full.reshape(seq_count, key_len, HEADS, DH)
    scores = jnp.einsum(
        "sqhd,skhd->shqk", query_heads, key_heads, preferred_element_type=jnp.float32
    )
    row_pos = first_pos + jnp.arange(query_heads.shape[1], dtype=jnp.int32)
    col_pos = jnp.arange(key_len, dtype=jnp.int32)
    allowed = row_pos[:, None] >= col_pos[None, :]
    return (jnp.where(allowed, scores, -1e30), key_heads)


def micro_step(tokens, cotangent, shards, forward_weights):
    (
        w_query,
        w_key,
        w_value,
        w_out,
        w_up,
        w_down,
        b_query,
        b_value,
        b_out,
        b_up,
        b_down,
        gain_one,
        shift_one,
        gain_two,
        shift_two,
    ) = forward_weights
    seq_count, block_rows, width = tokens.shape
    query_scale = DH ** (-0.5)
    first_pos = lax.axis_index("ctx") * block_rows
    gain_one32, shift_one32 = (gain_one.astype(jnp.float32), shift_one.astype(jnp.float32))
    gain_two32, shift_two32 = (gain_two.astype(jnp.float32), shift_two.astype(jnp.float32))
    tokens32 = tokens.astype(jnp.float32)
    normed = layer_norm(tokens32, gain_one32, shift_one32).astype(jnp.bfloat16)
    queries = ((project(normed, w_query) + b_query.astype(jnp.float32)) * query_scale).astype(
        jnp.bfloat16
    )
    keys_local = project(normed, w_key).astype(jnp.bfloat16)
    values_local = (project(normed, w_value) + b_value.astype(jnp.float32)).astype(jnp.bfloat16)
    key_full, value_full = (
        lax.all_gather(keys_local, "ctx", axis=1, tiled=True),
        lax.all_gather(values_local, "ctx", axis=1, tiled=True),
    )
    query_heads = queries.reshape(seq_count, block_rows, HEADS, DH)
    scores, key_heads = masked_scores(query_heads, key_full, first_pos)
    row_max = jnp.max(scores, axis=-1, keepdims=True)
    exp_scores = jnp.exp(scores - row_max)
    row_total = jnp.sum(exp_scores, axis=-1, keepdims=True)
    probs_low = (exp_scores / row_total).astype(jnp.bfloat16)
    value_heads = value_full.reshape(seq_count, value_full.shape[1], HEADS, DH)
    mixed_heads = jnp.einsum(
        "shqk,skhd->sqhd", probs_low, value_heads, preferred_element_type=jnp.float32
    ).reshape(seq_count, block_rows, width)
    mixed_heads = mixed_heads.astype(jnp.bfloat16)
    residual = tokens32 + project(mixed_heads, w_out) + b_out.astype(jnp.float32)
    normed_two = layer_norm(residual, gain_two32, shift_two32).astype(jnp.bfloat16)
    hidden_pre = project(normed_two, w_up) + b_up.astype(jnp.float32)
    active = gelu_tanh(hidden_pre).astype(jnp.bfloat16)
    output = (residual + project(active, w_down) + b_down.astype(jnp.float32)).astype(jnp.bfloat16)
    back_weights = (
        lax.all_gather(shards[0], ("dp", "ctx"), axis=0, tiled=True),
        lax.all_gather(shards[1], ("dp", "ctx"), axis=0, tiled=True),
        lax.all_gather(shards[2], ("dp", "ctx"), axis=0, tiled=True),
        lax.all_gather(shards[3], ("dp", "ctx"), axis=0, tiled=True),
        lax.all_gather(shards[4], ("dp", "ctx"), axis=0, tiled=True),
        lax.all_gather(shards[5], ("dp", "ctx"), axis=0, tiled=True),
        lax.all_gather(shards[6], ("dp", "ctx"), axis=0, tiled=True),
        lax.all_gather(shards[7], ("dp", "ctx"), axis=0, tiled=True),
        lax.all_gather(shards[8], ("dp", "ctx"), axis=0, tiled=True),
        lax.all_gather(shards[9], ("dp", "ctx"), axis=0, tiled=True),
        lax.all_gather(shards[10], ("dp", "ctx"), axis=0, tiled=True),
        lax.all_gather(shards[11], ("dp", "ctx"), axis=0, tiled=True),
        lax.all_gather(shards[12], ("dp", "ctx"), axis=0, tiled=True),
        lax.all_gather(shards[13], ("dp", "ctx"), axis=0, tiled=True),
        lax.all_gather(shards[14], ("dp", "ctx"), axis=0, tiled=True),
    )
    w_query, w_key, w_value, w_out, w_up, w_down = back_weights[:6]
    grad_active = project_back(cotangent, w_down)
    _, gelu_pull = jax.vjp(gelu_tanh, hidden_pre)
    grad_pre = gelu_pull(grad_active)[0].astype(jnp.bfloat16)
    grad_normed_two = project_back(grad_pre, w_up)
    _, norm_pull_two = jax.vjp(layer_norm, residual, gain_two32, shift_two32)
    grad_res_part, grad_gain_two, grad_shift_two = norm_pull_two(grad_normed_two)
    grad_residual = cotangent.astype(jnp.float32) + grad_res_part
    grad_branch = grad_residual.astype(jnp.bfloat16)
    grad_mixed = project_back(grad_branch, w_out).astype(jnp.bfloat16)
    key_full, value_full = (
        lax.all_gather(keys_local, "ctx", axis=1, tiled=True),
        lax.all_gather(values_local, "ctx", axis=1, tiled=True),
    )
    value_heads = value_full.reshape(seq_count, value_full.shape[1], HEADS, DH)
    scores, key_heads = masked_scores(query_heads, key_full, first_pos)
    probs = jnp.exp(scores - row_max) / row_total
    probs_low = probs.astype(jnp.bfloat16)
    grad_heads = grad_mixed.reshape(seq_count, block_rows, HEADS, DH)
    grad_probs = jnp.einsum(
        "sqhd,skhd->shqk", grad_heads, value_heads, preferred_element_type=jnp.float32
    )
    inner_rows = jnp.sum(probs * grad_probs, axis=-1, keepdims=True)
    grad_scores = (probs * (grad_probs - inner_rows)).astype(jnp.bfloat16)
    grad_queries = jnp.einsum(
        "shqk,skhd->sqhd", grad_scores, key_heads, preferred_element_type=jnp.float32
    )
    grad_queries = grad_queries.reshape(seq_count, block_rows, width).astype(jnp.bfloat16)
    query_grad = grad_queries * query_scale

    def key_terms(first_row, row_count):
        score_part = lax.dynamic_slice_in_dim(grad_scores, first_row, row_count, 3)
        prob_part = lax.dynamic_slice_in_dim(probs_low, first_row, row_count, 3)
        key_part = jnp.einsum(
            "shqk,sqhd->kshd", score_part, query_heads, preferred_element_type=jnp.float32
        )
        value_part = jnp.einsum(
            "shqk,sqhd->kshd", prob_part, grad_heads, preferred_element_type=jnp.float32
        )
        return jnp.concatenate(
            (
                key_part.reshape(row_count, seq_count, width),
                value_part.reshape(row_count, seq_count, width),
            ),
            axis=2,
        )

    cycle_size = lax.axis_size("ctx")
    own_index = lax.axis_index("ctx")

    def carry_step(step, carried):
        holder = (own_index - step) % cycle_size
        carried = carried + key_terms(holder * block_rows, block_rows)
        return shifted(carried.astype(jnp.bfloat16), "ctx", 1).astype(carried.dtype)

    start_sums = jnp.zeros((block_rows, seq_count, 2 * width), jnp.float32)
    key_sums = lax.fori_loop(0, cycle_size, carry_step, start_sums)
    key_sums = jnp.transpose(key_sums, (1, 0, 2))
    grad_keys = key_sums[:, :, :width].astype(jnp.bfloat16)
    grad_values = key_sums[:, :, width:].astype(jnp.bfloat16)
    grad_normed = (
        project_back(query_grad, w_query)
        + project_back(grad_keys, w_key)
        + project_back(grad_values, w_value)
    )
    _, norm_pull_one = jax.vjp(layer_norm, tokens32, gain_one32, shift_one32)
    grad_tok_part, grad_gain_one, grad_shift_one = norm_pull_one(grad_normed)
    grad_tokens = grad_residual + grad_tok_part
    small_grads = (grad_gain_one, grad_shift_one, grad_gain_two, grad_shift_two)
    operands = (
        normed,
        query_grad,
        grad_keys,
        grad_values,
        mixed_heads,
        grad_branch,
        normed_two,
        grad_pre,
        active,
        cotangent,
    )
    return (output, grad_tokens, small_grads, operands)


def owner_sum(grads):
    dp_count = lax.axis_size("dp")
    ctx_count = lax.axis_size("ctx")
    blocks = tuple((grad_part.reshape(dp_count, ctx_count, -1) for grad_part in grads))
    first_section = jax.tree.map(
        lambda part, own: part.astype(own.dtype),
        lax.all_to_all(as_sent(blocks), "ctx", split_axis=1, concat_axis=1, tiled=True),
        blocks,
    )
    partial_sums = tuple((jnp.sum(piece, axis=1, keepdims=True) for piece in first_section))
    second_section = jax.tree.map(
        lambda part, own: part.astype(own.dtype),
        lax.all_to_all(as_sent(partial_sums), "dp", split_axis=0, concat_axis=0, tiled=True),
        partial_sums,
    )
    owned = []
    for grad_part, piece in zip(grads, second_section):
        summed = jnp.sum(piece, axis=(0, 1))
        row_count = grad_part.shape[0] // (dp_count * ctx_count)
        owned.append(summed.reshape((row_count,) + grad_part.shape[1:]))
    return owned


def on_device(
    tokens_in,
    out_grad,
    w_query,
    w_key,
    w_value,
    w_out,
    w_up,
    w_down,
    b_query,
    b_value,
    b_out,
    b_up,
    b_down,
    norm1_gain,
    norm1_shift,
    norm2_gain,
    norm2_shift,
):
    shards = (
        w_query,
        w_key,
        w_value,
        w_out,
        w_up,
        w_down,
        b_query,
        b_value,
        b_out,
        b_up,
        b_down,
        norm1_gain,
        norm1_shift,
        norm2_gain,
        norm2_shift,
    )
    per_micro = tokens_in.shape[0] // MICRO
    outputs = []
    grads_in = []
    operand_lists = []
    small_total = None
    for micro_index in range(MICRO):
        lower = micro_index * per_micro
        tokens = tokens_in[lower : lower + per_micro]
        cotangent = out_grad[lower : lower + per_micro]
        forward_weights = (
            lax.all_gather(shards[0], ("dp", "ctx"), axis=0, tiled=True),
            lax.all_gather(shards[1], ("dp", "ctx"), axis=0, tiled=True),
            lax.all_gather(shards[2], ("dp", "ctx"), axis=0, tiled=True),
            lax.all_gather(shards[3], ("dp", "ctx"), axis=0, tiled=True),
            lax.all_gather(shards[4], ("dp", "ctx"), axis=0, tiled=True),
            lax.all_gather(shards[5], ("dp", "ctx"), axis=0, tiled=True),
            lax.all_gather(shards[6], ("dp", "ctx"), axis=0, tiled=True),
            lax.all_gather(shards[7], ("dp", "ctx"), axis=0, tiled=True),
            lax.all_gather(shards[8], ("dp", "ctx"), axis=0, tiled=True),
            lax.all_gather(shards[9], ("dp", "ctx"), axis=0, tiled=True),
            lax.all_gather(shards[10], ("dp", "ctx"), axis=0, tiled=True),
            lax.all_gather(shards[11], ("dp", "ctx"), axis=0, tiled=True),
            lax.all_gather(shards[12], ("dp", "ctx"), axis=0, tiled=True),
            lax.all_gather(shards[13], ("dp", "ctx"), axis=0, tiled=True),
            lax.all_gather(shards[14], ("dp", "ctx"), axis=0, tiled=True),
        )
        output, grad_tokens, small_grads, operands = micro_step(
            tokens, cotangent, shards, forward_weights
        )
        outputs.append(output)
        grads_in.append(grad_tokens)
        operand_lists.append(operands)
        if small_total is None:
            small_total = small_grads
        else:
            small_total = tuple(
                (total_grad + update for total_grad, update in zip(small_total, small_grads))
            )
    joined = tuple(
        (jnp.concatenate([entry[index] for entry in operand_lists], axis=0) for index in range(10))
    )
    (
        normed,
        query_grad,
        grad_keys,
        grad_values,
        mixed_heads,
        grad_branch,
        normed_two,
        grad_pre,
        active,
        cotangent,
    ) = joined
    grads = (
        weight_grad(normed, query_grad),
        weight_grad(normed, grad_keys),
        weight_grad(normed, grad_values),
        weight_grad(mixed_heads, grad_branch),
        weight_grad(normed_two, grad_pre),
        weight_grad(active, cotangent),
        column_sum(query_grad),
        column_sum(grad_values),
        column_sum(grad_branch),
        column_sum(grad_pre),
        column_sum(cotangent),
        small_total[0],
        small_total[1],
        small_total[2],
        small_total[3],
    )
    owned = owner_sum(grads)
    layer_out = jnp.concatenate(outputs, axis=0)
    grad_tokens_all = jnp.concatenate(grads_in, axis=0)
    return (
        layer_out,
        grad_tokens_all,
        owned[0],
        owned[1],
        owned[2],
        owned[3],
        owned[4],
        owned[5],
        owned[6],
        owned[7],
        owned[8],
        owned[9],
        owned[10],
        owned[11],
        owned[12],
        owned[13],
        owned[14],
    )


BF = jnp.bfloat16
F32 = jnp.float32
SMALL = 8


def other_core(value):
    return lax.ppermute(value, "core", [(0, 1), (1, 0)])


def other_x(value):
    return lax.ppermute(value, "x", [(0, 1), (1, 0)])


def other_y(value):
    return lax.ppermute(value, "y", [(0, 1), (1, 0)])


def other_z(value, by):
    return lax.ppermute(value, "z", [(i, i ^ by) for i in range(lax.axis_size("z"))])


def pair(bit, own, received):
    return jnp.stack((jnp.where(bit == 0, own, received), jnp.where(bit == 0, received, own)))


def pick(value, index, axis):
    return lax.dynamic_index_in_dim(value, index, axis, keepdims=False)


def in_order(index, pieces):
    level = list(pieces)
    bit = 0
    ordered = [p[None] for p in level]
    while len(ordered) > 1:
        flag = (index >> bit) & 1
        ordered = [
            jnp.concatenate(
                (jnp.where(flag == 0, a, b), jnp.where(flag == 0, b, a)), axis=0
            )
            for a, b in zip(ordered[::2], ordered[1::2])
        ]
        bit += 1
    return ordered[0]


def gather_plane(along_z, x, y):
    half = along_z.shape[0] // 2
    first, second = along_z[:half], along_z[half:]
    first = pair(x, first, other_x(first))
    second = pair(y, second, other_y(second))
    first = pair(y, first, other_y(first))
    second = pair(x, second, other_x(second))
    return jnp.concatenate((jnp.moveaxis(first, 2, 0).swapaxes(1, 2), jnp.moveaxis(second, 2, 0)))


def plus(kept, received):
    return kept.astype(F32) + received.astype(F32)


LIGHT = pl.CostEstimate(flops=0, bytes_accessed=1, transcendentals=0)
VMEM_LIMIT = 56 * 1024 * 1024
QUERY_BLOCK = 256


def lane_masks(dtype):
    lane = lax.broadcasted_iota(jnp.int32, (1, 2 * DH), 1)
    return [(lane < DH).astype(dtype), (lane >= DH).astype(dtype)]


def visible(key_count, query_block):
    key_pos = lax.broadcasted_iota(jnp.int32, (query_block, query_block), 0)
    query_pos = lax.broadcasted_iota(jnp.int32, (query_block, query_block), 1)
    return key_pos <= query_pos


def masked_tail(scores, allowed):
    key_count, query_block = scores.shape
    tail = jnp.where(allowed, scores[key_count - query_block :], -1e30)
    if key_count == query_block:
        return tail
    return jnp.concatenate((scores[: key_count - query_block], tail), axis=0)


def nt(left, right):
    return lax.dot_general(left, right, (((1,), (1,)), ((), ())), preferred_element_type=F32)


def nn(left, right):
    return lax.dot_general(left, right, (((1,), (0,)), ((), ())), preferred_element_type=F32)


def attend_kernel(q_ref, k_ref, v_ref, mixed_ref, lse_ref):
    length = q_ref.shape[0]
    masks = lane_masks(BF)
    allowed = visible(QUERY_BLOCK, QUERY_BLOCK)
    keys = k_ref[...]
    masked_keys = [keys * m for m in masks]
    v_t = v_ref[...].T
    row = lax.broadcasted_iota(jnp.int32, (2 * DH, 1), 0)
    values_t = [jnp.where(row < DH, v_t, jnp.zeros((), BF)), jnp.where(row >= DH, v_t, jnp.zeros((), BF))]
    for start in range(0, length, QUERY_BLOCK):
        stop = start + QUERY_BLOCK
        q = q_ref[start:stop, :]
        mixed_t = None
        for head in range(2):
            scores = masked_tail(nt(masked_keys[head][:stop], q), allowed)
            top = jnp.max(scores, axis=0, keepdims=True)
            powers = jnp.exp(scores - top)
            total = jnp.sum(powers, axis=0, keepdims=True)
            low = (powers * (1.0 / total)).astype(BF)
            part = nn(values_t[head][:, :stop], low)
            mixed_t = part if mixed_t is None else mixed_t + part
            lse_ref[0, head : head + 1, start:stop] = top + jnp.log(total)
        mixed_ref[start:stop, :] = mixed_t.T.astype(BF)


def attend_back_kernel(q_ref, k_ref, v_ref, g_ref, mixed_ref, lse_ref, gq_ref, gk_ref, gv_ref, ka, va):
    length = q_ref.shape[0]
    masks = lane_masks(BF)
    allowed = visible(QUERY_BLOCK, QUERY_BLOCK)
    keys, values = k_ref[...], v_ref[...]
    masked_keys = [keys * m for m in masks]
    masked_values = [values * m for m in masks]
    keys_t = [m.T for m in masked_keys]
    for start in range(length - QUERY_BLOCK, -1, -QUERY_BLOCK):
        stop = start + QUERY_BLOCK
        q, g = q_ref[start:stop, :], g_ref[start:stop, :]
        products = (g.astype(F32) * mixed_ref[start:stop, :].astype(F32)).T
        grad_q_t = None
        grad_k = grad_v = None
        for head in range(2):
            inner = jnp.sum(products[head * DH : (head + 1) * DH], axis=0, keepdims=True)
            scores = masked_tail(nt(masked_keys[head][:stop], q), allowed)
            probs = jnp.exp(scores - lse_ref[0, head : head + 1, start:stop])
            grad_probs = nt(masked_values[head][:stop], g)
            grad_scores = (probs * (grad_probs - inner)).astype(BF)
            part_v = nn(probs.astype(BF), g * masks[head])
            part_k = nn(grad_scores, q * masks[head])
            part_q = nn(keys_t[head][:, :stop], grad_scores)
            grad_v = part_v if head == 0 else grad_v + part_v
            grad_k = part_k if head == 0 else grad_k + part_k
            grad_q_t = part_q if head == 0 else grad_q_t + part_q
        gq_ref[start:stop, :] = grad_q_t.T.astype(BF)
        if stop == length:
            ka[...] = grad_k
            va[...] = grad_v
        else:
            ka[:stop, :] += grad_k
            va[:stop, :] += grad_v
    gk_ref[...] = ka[...].astype(BF)
    gv_ref[...] = va[...].astype(BF)


def attend(queries, keys, values):
    length, width = queries.shape
    pairs = width // (2 * DH)
    block = pl.BlockSpec((length, 2 * DH), lambda i: (0, i))
    return pl.pallas_call(
        attend_kernel,
        grid=(pairs,),
        in_specs=[block] * 3,
        out_specs=[block, pl.BlockSpec((1, 2, length), lambda i: (i, 0, 0))],
        out_shape=[
            jax.ShapeDtypeStruct((length, width), BF),
            jax.ShapeDtypeStruct((pairs, 2, length), F32),
        ],
        compiler_params=pltpu.CompilerParams(vmem_limit_bytes=VMEM_LIMIT),
        cost_estimate=LIGHT,
        name="attend",
    )(queries, keys, values)


def attend_back(queries, keys, values, mixed, lse, grad_mixed, pair_index, pairs):
    length = queries.shape[0]
    block = pl.BlockSpec((length, 2 * DH), lambda i: (0, i + pair_index))
    out_block = pl.BlockSpec((length, 2 * DH), lambda i: (0, i))
    width = pairs * 2 * DH
    return pl.pallas_call(
        attend_back_kernel,
        grid=(pairs,),
        in_specs=[block] * 5 + [pl.BlockSpec((1, 2, length), lambda i: (i + pair_index, 0, 0))],
        out_specs=[out_block] * 3,
        out_shape=[jax.ShapeDtypeStruct((length, width), BF)] * 3,
        scratch_shapes=[pltpu.VMEM((length, 2 * DH), F32)] * 2,
        compiler_params=pltpu.CompilerParams(vmem_limit_bytes=VMEM_LIMIT),
        cost_estimate=LIGHT,
        name="attend_back",
    )(queries, keys, values, grad_mixed, mixed, lse)


def position_blocks(core, block):
    return [
        (b, own, pl.multiple_of(b * 2 * block + (core if own else 1 - core) * block, block))
        for b in range(2)
        for own in (True, False)
    ]


def normalise(values):
    centre = values - jnp.mean(values, axis=-1, keepdims=True)
    spread = jnp.mean(centre * centre, axis=-1, keepdims=True)
    rate = lax.rsqrt(spread + 1e-05)
    return centre * rate, rate


def normalise_back(unit, rate, gain, grad):
    scaled = grad * gain
    return rate * (
        scaled
        - jnp.mean(scaled, axis=-1, keepdims=True)
        - unit * jnp.mean(scaled * unit, axis=-1, keepdims=True)
    )


CORE, X, Y = range(3)
B_QUERY, B_VALUE, B_OUT, B_DOWN, GAIN1, SHIFT1, GAIN2, SHIFT2 = range(8)


def weight(ref, i):
    chips, _, width = ref.shape
    rows = width * 2 // chips
    return ref[:, i * rows : (i + 1) * rows, :].reshape(chips * rows, width)


def add_sums(ref, values):
    @pl.when(pl.program_id(0) == 0)
    def _():
        ref[...] = jnp.zeros(ref.shape, F32)

    for i, value in enumerate(values):
        ref[i : i + 1, :] += jnp.sum(value, axis=0, keepdims=True)


def enter_kernel(core_ref, mine_ref, other_ref, vec_ref, half_ref, w_ref, n_ref, q_ref, k_ref, v_ref):
    core = core_ref[0]
    block = mine_ref.shape[0] // 2
    for b, own, row in position_blocks(core, block):
        tokens = (mine_ref if own else other_ref)[b * block : (b + 1) * block, :].astype(F32)
        unit, _ = normalise(tokens)
        normed = (unit * vec_ref[GAIN1 : GAIN1 + 1, :] + vec_ref[SHIFT1 : SHIFT1 + 1, :]).astype(BF)
        rows = pl.ds(row, block)
        n_ref[rows, :] = normed
        q = (nn(normed, weight(w_ref, 0)) + half_ref[B_QUERY : B_QUERY + 1, :]) * DH ** (-0.5)
        q_ref[rows, :] = q.astype(BF)
        k_ref[rows, :] = nn(normed, weight(w_ref, 1)).astype(BF)
        v_ref[rows, :] = (nn(normed, weight(w_ref, 2)) + half_ref[B_VALUE : B_VALUE + 1, :]).astype(BF)


def out_kernel(core_ref, mixed_ref, w_ref, mine_ref, other_ref):
    block = mine_ref.shape[0] // 2
    for b, own, row in position_blocks(core_ref[0], block):
        part = nn(mixed_ref[pl.ds(row, block), :], w_ref[...])
        ref = mine_ref if own else other_ref
        ref[b * block : (b + 1) * block, :] = part.astype(ref.dtype)


def middle_kernel(tokens_ref, part_ref, received_ref, vec_ref, residual_ref, n_ref):
    residual = (
        tokens_ref[...].astype(F32)
        + part_ref[...]
        + received_ref[...].astype(F32)
        + vec_ref[B_OUT : B_OUT + 1, :]
    )
    unit, _ = normalise(residual)
    residual_ref[...] = residual
    n_ref[...] = (unit * vec_ref[GAIN2 : GAIN2 + 1, :] + vec_ref[SHIFT2 : SHIFT2 + 1, :]).astype(BF)


def middle_back_kernel(residual_ref, gn_ref, gn_received_ref, g_ref, vec_ref, gr_ref, branch_ref, sums_ref):
    unit, rate = normalise(residual_ref[...])
    grad_normed = gn_ref[...] + gn_received_ref[...].astype(F32)
    cotangent = g_ref[...].astype(F32)
    grad = cotangent + normalise_back(unit, rate, vec_ref[GAIN2 : GAIN2 + 1, :], grad_normed)
    gr_ref[...] = grad
    branch = grad.astype(BF)
    branch_ref[...] = branch
    add_sums(sums_ref, (branch.astype(F32), cotangent, grad_normed * unit, grad_normed))


def mixed_back_kernel(core_ref, mixed_ref, mine_ref, other_ref, w_ref, gm_ref, gw_ref):
    block = mine_ref.shape[0] // 2
    total = None
    for b, own, row in position_blocks(core_ref[0], block):
        branch = (mine_ref if own else other_ref)[b * block : (b + 1) * block, :]
        rows = pl.ds(row, block)
        gm_ref[rows, :] = nt(branch, w_ref[...]).astype(BF)
        part = nn(mixed_ref[rows, :].T, branch)
        total = part if total is None else total + part
    gw_ref[...] = total.astype(BF)


def weight_back_kernel(
    place_ref, n_ref, q_ref, k_ref, v_ref, left_keep, left_send, right_keep, right_send, sums_ref, by_y, by_x
):
    x, y = place_ref[X], place_ref[Y]
    n_t = n_ref[...].T
    rows = by_y.shape[2]
    grads = [q_ref[...] * jnp.asarray(DH ** (-0.5), BF), k_ref[...], v_ref[...]]
    for i in range(2):
        by_y[...] = nn(n_t, grads[i]).astype(BF).reshape(by_y.shape)
        part = slice(i * rows, (i + 1) * rows)
        left_keep[:, part, :] = by_y[:, pl.ds(y, 1)].reshape(-1, rows, by_y.shape[3])
        left_send[:, part, :] = by_y[:, pl.ds(1 - y, 1)].reshape(-1, rows, by_y.shape[3])
    by_x[...] = nn(n_t, grads[2]).astype(BF).reshape(by_x.shape)
    right_keep[...] = by_x[:, pl.ds(x, 1)].reshape(right_keep.shape)
    right_send[...] = by_x[:, pl.ds(1 - x, 1)].reshape(right_send.shape)
    half = q_ref.shape[1]
    side = lax.broadcasted_iota(jnp.int32, (1, 2 * half), 1) >= half
    for i, grad in enumerate((grads[0], grads[2])):
        total = jnp.sum(grad.astype(F32), axis=0, keepdims=True)
        total = jnp.concatenate((total, total), axis=1)
        sums_ref[i : i + 1, :] = jnp.where(side == (place_ref[CORE] == 1), total, 0.0)


def enter_back_kernel(place_ref, q_ref, k_ref, v_ref, w_ref, mine_ref, other_ref):
    block = mine_ref.shape[0] // 2
    for b, own, row in position_blocks(place_ref[CORE], block):
        rows = pl.ds(row, block)
        part = (
            nt(q_ref[rows, :] * jnp.asarray(DH ** (-0.5), BF), weight(w_ref, 0))
            + nt(k_ref[rows, :], weight(w_ref, 1))
            + nt(v_ref[rows, :], weight(w_ref, 2))
        )
        ref = mine_ref if own else other_ref
        ref[b * block : (b + 1) * block, :] = part.astype(ref.dtype)


def leave_kernel(tokens_ref, gn_ref, gn_received_ref, gr_ref, vec_ref, gt_ref, sums_ref):
    unit, rate = normalise(tokens_ref[...].astype(F32))
    grad_normed = gn_ref[...] + gn_received_ref[...].astype(F32)
    gt_ref[...] = gr_ref[...] + normalise_back(unit, rate, vec_ref[GAIN1 : GAIN1 + 1, :], grad_normed)
    add_sums(sums_ref, (grad_normed * unit, grad_normed))


def shape(dims, dtype):
    return jax.ShapeDtypeStruct(dims, dtype)


def whole_call(kernel, outs, *args, flops=0, scalars=0, scratch=()):
    in_specs = [
        pl.BlockSpec(memory_space=pltpu.SMEM if i < scalars else pltpu.VMEM)
        for i in range(len(args))
    ]
    moved = sum(a.size * a.dtype.itemsize for a in list(args) + outs)
    return pl.pallas_call(
        kernel,
        in_specs=in_specs,
        out_specs=[pl.BlockSpec(memory_space=pltpu.VMEM)] * len(outs),
        out_shape=outs,
        scratch_shapes=list(scratch),
        compiler_params=pltpu.CompilerParams(vmem_limit_bytes=VMEM_LIMIT),
        cost_estimate=LIGHT,
        name=kernel.__name__,
    )(*args)


def row_call(kernel, outs, sums, *args):
    length, width = args[0].shape
    block = length // 2
    rows = pl.BlockSpec((block, width), lambda i: (i, 0))
    out_shape = [shape((length, width), dtype) for dtype in outs]
    out_specs = [rows] * len(outs)
    if sums:
        out_shape.append(shape((sums, width), F32))
        out_specs.append(pl.BlockSpec((sums, width), lambda i: (0, 0)))
    moved = sum(a.size * a.dtype.itemsize for a in list(args) + out_shape)
    return pl.pallas_call(
        kernel,
        grid=(2,),
        in_specs=[rows] * (len(args) - 1) + [pl.BlockSpec(args[-1].shape, lambda i: (0, 0))],
        out_specs=out_specs,
        out_shape=out_shape,
        compiler_params=pltpu.CompilerParams(vmem_limit_bytes=VMEM_LIMIT),
        cost_estimate=LIGHT,
        name=kernel.__name__,
    )(*args)


def hidden_kernel(
    place_ref, n_mine, n_other, g_mine, g_other, up_ref, down_ref, bias_ref,
    y_mine, y_other, gn_mine, gn_other, up_keep, up_send, down_keep, down_send, gb_ref,
    n_t, y_sum, gn_sum, up_all, down_all,
):
    step = pl.program_id(0)
    length = n_mine.shape[0]

    @pl.when(step == 0)
    def _():
        n_t[:, :length] = n_mine[...].T
        n_t[:, length:] = n_other[...].T
        for ref in (y_mine, gn_mine, y_sum, gn_sum):
            ref[...] = jnp.zeros(ref.shape, F32)

    up = up_ref[...].reshape(-1, up_ref.shape[2])
    down = down_ref[...].reshape(-1, down_ref.shape[2])
    grad_up = grad_down = bias_sum = None
    for part, (n_ref, g_ref, y_ref, gn_ref) in enumerate(
        ((n_mine, g_mine, y_mine, gn_mine), (n_other, g_other, y_sum, gn_sum))
    ):
        n, g = n_ref[...], g_ref[...]
        pre = nn(n, up) + bias_ref[0]
        square = pre * pre
        bent = jnp.tanh(pre * (0.7978845608028654 + 0.7978845608028654 * 0.044715 * square))
        half = 0.5 + 0.5 * bent
        active = (pre * half).astype(BF)
        rise = pre * (2 * 0.7978845608028654 + 6 * 0.7978845608028654 * 0.044715 * square)
        slope = half * (1.0 + (1.0 - half) * rise)
        grad_pre = (nt(g, down) * slope).astype(BF)
        y_ref[...] += nn(active, down)
        gn_ref[...] += nt(grad_pre, up)
        part_up = nn(n_t[:, part * length : (part + 1) * length], grad_pre)
        part_down = lax.dot_general(active, g, (((0,), (0,)), ((), ())), preferred_element_type=F32)
        part_bias = jnp.sum(grad_pre.astype(F32), axis=0, keepdims=True)
        grad_up = part_up if part == 0 else grad_up + part_up
        grad_down = part_down if part == 0 else grad_down + part_down
        bias_sum = part_bias if part == 0 else bias_sum + part_bias
    x, y = place_ref[X], place_ref[Y]
    up_all[...] = grad_up.astype(BF).reshape(up_all.shape)
    up_keep[...] = up_all[:, pl.ds(y, 1)].reshape(up_keep.shape)
    up_send[...] = up_all[:, pl.ds(1 - y, 1)].reshape(up_send.shape)
    down_all[...] = grad_down.astype(BF).reshape(down_all.shape)
    down_keep[...] = down_all[:, pl.ds(x, 1)].reshape(down_keep.shape)
    down_send[...] = down_all[:, pl.ds(1 - x, 1)].reshape(down_send.shape)
    gb_ref[0] = bias_sum

    @pl.when(step == pl.num_programs(0) - 1)
    def _():
        y_other[...] = y_sum[...].astype(BF)
        gn_other[...] = gn_sum[...].astype(BF)


def feed_forward(place, n_mine, n_other, g_mine, g_other, late, bias, hidden_rows):
    length, width = n_mine.shape
    chips = late.shape[0]
    steps = 2
    z_count = chips // 4
    z_step = z_count // steps
    tile = chips * hidden_rows // steps
    up_rows = width // chips
    per_half = steps // 2
    down_chips = chips // steps
    full = pl.BlockSpec((length, width), lambda i: (0, 0))
    hidden = tile * steps
    return pl.pallas_call(
        hidden_kernel,
        grid=(steps,),
        in_specs=[pl.BlockSpec(memory_space=pltpu.SMEM)] + [full] * 4
        + [
            pl.BlockSpec((chips, up_rows, tile), lambda i: (0, i // per_half, i % per_half)),
            pl.BlockSpec((down_chips, hidden_rows, width), lambda i: (i, 1, 0)),
            pl.BlockSpec((1, 1, tile), lambda i: (i, 0, 0)),
        ],
        out_specs=[full] * 4
        + [
            pl.BlockSpec((chips // 2, up_rows, tile), lambda i: (0, 0, i)),
            pl.BlockSpec((chips // 2, up_rows, tile), lambda i: (0, 0, i)),
            pl.BlockSpec((z_step, 2, hidden_rows, width), lambda i: (i, 0, 0, 0)),
            pl.BlockSpec((z_step, 2, hidden_rows, width), lambda i: (i, 0, 0, 0)),
            pl.BlockSpec((1, 1, tile), lambda i: (i, 0, 0)),
        ],
        out_shape=[
            shape((length, width), F32),
            shape((length, width), BF),
            shape((length, width), F32),
            shape((length, width), BF),
            shape((chips // 2, up_rows, hidden), BF),
            shape((chips // 2, up_rows, hidden), BF),
            shape((z_count, 2, hidden_rows, width), BF),
            shape((z_count, 2, hidden_rows, width), BF),
            shape((steps, 1, tile), F32),
        ],
        scratch_shapes=[
            pltpu.VMEM((width, 2 * length), BF),
            pltpu.VMEM((length, width), F32),
            pltpu.VMEM((length, width), F32),
            pltpu.VMEM((chips // 2, 2, up_rows, tile), BF),
            pltpu.VMEM((z_step, 2, 2, hidden_rows, width), BF),
        ],
        compiler_params=pltpu.CompilerParams(vmem_limit_bytes=VMEM_LIMIT),
        cost_estimate=LIGHT,
        name="feed_forward",
    )(place, n_mine, n_other, g_mine, g_other, late, late, bias.reshape(steps, 1, tile))


def chip_step(
    tokens_in,
    out_grad,
    w_query,
    w_key,
    w_value,
    w_out,
    w_up,
    w_down,
    b_query,
    b_value,
    b_out,
    b_up,
    b_down,
    norm1_gain,
    norm1_shift,
    norm2_gain,
    norm2_shift,
):
    z, x, y, core = (lax.axis_index(name) for name in ("z", "x", "y", "core"))
    z_count = lax.axis_size("z")
    chips = z_count * 4
    half_chips = chips // 2
    _, block, width = tokens_in.shape
    half = width // 2
    rows = w_query.shape[0]
    hidden_rows = w_down.shape[0]
    hidden = hidden_rows * chips

    def own_positions(value):
        return pair(y, pick(value, y, 0), other_y(pick(value, 1 - y, 0))).reshape(2 * block, width)

    three = jnp.stack((w_query, w_key, w_value)).reshape(3, rows, 2, half)
    vectors = (
        b_query, b_value, b_out, b_down, norm1_gain, norm1_shift, norm2_gain, norm2_shift, b_up
    )
    small = jnp.concatenate(vectors)
    unit_rows = 3 * rows + SMALL
    small_rows = jnp.zeros((SMALL, half), BF).at[0, : small.shape[0]].set(small)
    own = jnp.concatenate((pick(three, core, 2).reshape(3 * rows, half), small_rows))
    unit = pair(
        core,
        own,
        other_core(
            jnp.concatenate((pick(three, 1 - core, 2).reshape(3 * rows, half), small_rows))
        ),
    )
    up_parts = w_up.reshape(rows, chips, 2, hidden_rows)
    up_unit = pair(
        core,
        pick(up_parts, core, 2).reshape(rows, hidden),
        other_core(pick(up_parts, 1 - core, 2).reshape(rows, hidden)),
    )
    up_unit = up_unit.reshape(2 * rows, 2, width)
    late = jnp.concatenate((up_unit[:, 0], up_unit[:, 1], w_down))
    late = lax.all_gather(late, ("z", "x", "y"), axis=0, tiled=False)
    threes = unit[:, : 3 * rows].reshape(2, 3, rows, half).swapaxes(0, 1).reshape(6 * rows, half)
    unit = jnp.concatenate(
        (threes, unit[:, 3 * rows :].reshape(2 * SMALL, half), w_out[:, :half], w_out[:, half:])
    )
    pieces = [unit] + [other_z(unit, k) for k in range(1, z_count)]
    both = jnp.stack((pick(tokens_in, y, 0), pick(out_grad, y, 0)))
    both_from = other_y(jnp.stack((pick(tokens_in, 1 - y, 0), pick(out_grad, 1 - y, 0))))
    pieces, both_from = lax.optimization_barrier((pieces, both_from))
    both = pair(y, both, both_from).swapaxes(0, 1).reshape(2, 2 * block, width)
    mine, grad_mine = both[0], both[1]
    other, grad_other = other_core(mine), other_core(grad_mine)
    place = jnp.stack((core, x, y)).astype(jnp.int32)
    gathered = gather_plane(in_order(z, pieces), x, y)
    out_parts = jnp.concatenate(
        (gathered[..., 2 * unit_rows : 2 * unit_rows + rows, :], gathered[..., 2 * unit_rows + rows :, :]),
        axis=-1,
    ).reshape(2, half_chips, rows, width)
    out_c = (
        pair(core, pick(out_parts, core, 0), other_core(pick(out_parts, 1 - core, 0)))
        .swapaxes(0, 1)
        .reshape(half, width)
    )
    gathered = gathered.reshape(chips, -1, half)
    small_all = gathered[:, 6 * rows : 6 * rows + 2 * SMALL].reshape(chips * 2, SMALL, half)
    small_all = small_all[:, 0, : small.shape[0]]
    vectors = small_all[:, : 8 * rows].reshape(chips * 2, 8, rows).swapaxes(0, 1)
    vectors = vectors.reshape(8, width).astype(F32)
    halves = pick(vectors.reshape(8, 2, half), core, 1)
    bias_u = pick(small_all[:, 8 * rows :].reshape(chips, 2, hidden_rows), core, 1)
    bias_u = bias_u.reshape(hidden).astype(F32)

    length = 4 * block
    heads_shape = shape((length, half), BF)
    normed, queries, keys, values = whole_call(
        enter_kernel,
        [shape((length, width), BF)] + [heads_shape] * 3,
        place, mine, other, vectors, halves, gathered,
        flops=6 * length * width * half, scalars=1,
    )
    mixed, lse = attend(queries, keys, values)
    mine_shape = shape((2 * block, width), F32)
    sent_shape = shape((2 * block, width), BF)
    part, to_other = whole_call(
        out_kernel, [mine_shape, sent_shape], place, mixed, out_c,
        flops=2 * length * width * half, scalars=1,
    )
    residual, normed2 = row_call(middle_kernel, (F32, BF), 0, mine, part, other_core(to_other), vectors)
    late, normed2 = lax.optimization_barrier((late, normed2))
    y_mine, y_other, gn_mine, gn_other, up_keep, up_send, down_keep, down_send, up_sums = feed_forward(
        place, normed2, other_core(normed2), grad_mine, grad_other, late, bias_u, hidden_rows
    )

    up_from, down_from = other_y(up_send), other_x(down_send)
    grad_residual, branch, sums2 = row_call(
        middle_back_kernel, (F32, BF), 4, residual, gn_mine, other_core(gn_other), grad_mine, vectors
    )
    grad_mixed, grad_out = whole_call(
        mixed_back_kernel, [heads_shape, shape((half, width), BF)],
        place, mixed, branch, other_core(branch), out_c,
        flops=4 * length * width * half, scalars=1,
    )
    grad_out = grad_out.reshape(half_chips, 2, rows, width)
    grad_out = pair(
        core,
        pick(grad_out, core, 1),
        other_core(pick(grad_out, 1 - core, 1)),
    ).reshape(z_count, 2, 2, rows, width)
    grads = attend_back(
        queries, keys, values, mixed, lse, grad_mixed, 0, half // (2 * DH)
    )
    up_from, down_from, grads = lax.optimization_barrier((up_from, down_from, grads))
    ups = plus(up_keep, up_from).reshape(z_count, 2, 2 * rows, hidden)
    downs = plus(down_keep, down_from)
    up_send, down_send = pick(ups, 1 - x, 1).astype(BF), pick(downs, 1 - y, 1).astype(BF)
    up_send, down_send, grads = lax.optimization_barrier((up_send, down_send, grads))
    up_from, down_from, out_from = other_x(up_send), other_y(down_send), other_x(pick(grad_out, 1 - x, 1))
    left_shape = shape((2 * z_count, 4 * rows, half), BF)
    right_shape = shape((z_count, 2, 2 * rows, half), BF)
    left_keep, left_send, right_keep, right_send, sums_heads = whole_call(
        weight_back_kernel,
        [left_shape] * 2 + [right_shape] * 2 + [shape((2, width), F32)],
        place, normed, *grads,
        flops=6 * length * width * half, scalars=1,
        scratch=(
            pltpu.VMEM((2 * z_count, 2, 2 * rows, half), BF),
            pltpu.VMEM((z_count, 2, 2, 2 * rows, half), BF),
        ),
    )
    left_send, right_send, grads, y_mine, y_other = lax.optimization_barrier(
        (left_send, right_send, grads, y_mine, y_other)
    )
    left_from, right_from = other_y(left_send), other_x(right_send)
    gn_mine, gn_other = whole_call(
        enter_back_kernel,
        [mine_shape, sent_shape],
        place, *grads, gathered,
        flops=6 * length * width * half, scalars=1,
    )
    up_from, down_from, out_from, gn_mine, gn_other = lax.optimization_barrier(
        (up_from, down_from, out_from, gn_mine, gn_other)
    )
    low, high = z & 1, z >> 1

    def first_z(value):
        value = value.reshape((z_count // 2, 2) + value.shape[1:])
        return pick(value, low, 1), other_z(pick(value, 1 - low, 1).astype(BF), 1)

    def second_z(value):
        return pick(value, high, 0), other_z(pick(value, 1 - high, 0).astype(BF), 2)

    gn_from = other_core(gn_other)
    ups = plus(pick(ups, x, 1), up_from)
    downs = plus(pick(downs, y, 1), down_from)
    outs = plus(pick(grad_out, x, 1), out_from)
    forward_kept, forward_from = first_z(
        jnp.concatenate((ups[..., :width], ups[..., width:], downs), axis=1)
    )
    left_from, right_from, gn_from = lax.optimization_barrier((left_from, right_from, gn_from))
    lefts = plus(left_keep, left_from).reshape(z_count, 2, 4 * rows, half)
    rights = plus(right_keep, right_from)
    rights = jnp.concatenate((rights, outs[..., :half], outs[..., half:]), axis=2)
    left_send, right_send = pick(lefts, 1 - x, 1).astype(BF), pick(rights, 1 - y, 1).astype(BF)
    left_send, right_send, gn_from = lax.optimization_barrier((left_send, right_send, gn_from))
    left_from, right_from = other_x(left_send), other_y(right_send)
    grad_tokens, sums1 = row_call(
        leave_kernel, (F32,), 2, mine, gn_mine, gn_from, grad_residual, vectors
    )
    output = residual + y_mine + other_core(y_other).astype(F32) + vectors[B_DOWN]
    output = output.astype(BF).reshape(2, block, width)
    grad_tokens = grad_tokens.reshape(2, block, width)
    to_y = jnp.concatenate((pick(output, 1 - y, 0), pick(grad_tokens, 1 - y, 0).astype(BF)))
    forward_from, to_y = lax.optimization_barrier((forward_from, to_y))
    from_y = other_y(to_y)
    forward_kept, forward_from = second_z(plus(forward_kept, forward_from))

    left_from, right_from, sums1 = lax.optimization_barrier((left_from, right_from, sums1))
    small_grads = jnp.concatenate((sums_heads, sums2, sums1, up_sums.reshape(2, width)))
    small_grads = small_grads + other_y(small_grads)
    small_grads = small_grads + other_x(small_grads)
    lefts = plus(pick(lefts, x, 1), left_from)
    rights = plus(pick(rights, y, 1), right_from)
    last, last_from = first_z(jnp.concatenate((lefts, rights), axis=1))
    last_from, small_grads = lax.optimization_barrier((last_from, small_grads))
    small_grads = small_grads + other_z(small_grads, 1)
    small_grads = small_grads + other_z(small_grads, 2)
    small_core = small_grads[:8] + other_core(small_grads[:8])
    last_from, forward_from = lax.optimization_barrier((last_from, forward_from))
    last, last_from = second_z(plus(last, last_from))
    forward_sum = plus(forward_kept, forward_from)
    last = plus(last, last_from)
    layer_out = pair(y, pick(output, y, 0), from_y[:block])
    grad_tokens = pair(y, pick(grad_tokens, y, 0), from_y[block:].astype(F32))

    up_mine = forward_sum[: 4 * rows].reshape(2, 2, rows, width)
    down_mine = forward_sum[4 * rows :]
    three_mine = last[: 6 * rows].reshape(3, 2, rows, half)
    out_mine = jnp.concatenate((last[6 * rows : 7 * rows], last[7 * rows : 8 * rows]), axis=1)
    up_from = other_core(pick(up_mine, 1 - core, 1))
    chip = (z * 2 + x) * 2 + y
    small_mine = lax.dynamic_slice_in_dim(small_core, (chip * 2 + core) * rows, rows, 1)
    up_bias = lax.dynamic_slice_in_dim(small_grads[8:].reshape(hidden), chip * hidden_rows, hidden_rows, 0)
    three_from = other_core(pick(three_mine, 1 - core, 1))
    three_out = pair(core, pick(three_mine, core, 1), three_from)
    up_out = pair(core, pick(up_mine, core, 1), up_from)
    up_out = up_out.reshape(2, 2, rows, half_chips, hidden_rows)
    up_out = jnp.transpose(up_out, (2, 1, 3, 0, 4)).reshape(rows, 2 * hidden)
    g_q, g_k, g_v = (jnp.concatenate((three_out[0, i], three_out[1, i]), axis=1) for i in range(3))
    g_small = [small_mine[i] for i in (0, 1, 2, 3, 6, 7, 4, 5)]
    return (
        layer_out,
        grad_tokens,
        g_q,
        g_k,
        g_v,
        out_mine,
        up_out,
        down_mine,
        g_small[0],
        g_small[1],
        g_small[2],
        up_bias,
        g_small[3],
        g_small[4],
        g_small[5],
        g_small[6],
        g_small[7],
    )


def solution(mesh):
    dp_count, ctx_count = mesh.shape["dp"], mesh.shape["ctx"]

    def run(*args):
        per_dp = args[0].shape[0] // dp_count
        if ctx_count == 4 and per_dp == 2 and dp_count == 8:
            devices = mesh.devices.reshape(dp_count // 2, 2, ctx_count // 2, 2)
            used = Mesh(devices, ("z", "x", "y", "core"))
            body, dp, ctx = chip_step, ("z", "x"), ("y", "core")
        else:
            used, body, dp, ctx = mesh, on_device, ("dp",), ("ctx",)
        tokens, matrix, bias = P(dp, ctx, None), P(dp + ctx, None), P(dp + ctx)
        return jax.shard_map(
            body,
            mesh=used,
            in_specs=(tokens,) * 2 + (matrix,) * 6 + (bias,) * 9,
            out_specs=(tokens,) * 2 + (matrix,) * 6 + (bias,) * 9,
            check_vma=False,
        )(*args)

    return run
```

profile of v0, /device:TPU:0, one launch (start us, length us, event | category | flops | bytes accessed | tf_op | source)
XLA Modules:
  0.0 276.2 jit_solution(16137400224174528698)
XLA Ops:
  7.2 1.1 reshape.219
  8.4 1.3 dynamic-slice_reduce_fusion.1
  13.9 2.7 collective-permute-start.4
  16.7 3.7 %collective-permute-start.3 = (bf16[208,384]{1,0:T(8,128)(2,1)S(1)}, bf16[208,384]{1,0:T(8,128)(2,1)S(1)}, u32[]{:S(2)}, u32[]{:S(2)}) collective-permute-start(bf16[208,384]{1,0:T(8,128)(2,1)S(1)} %pad_maximum_fusion.16), channel_id=1, source_target_pairs={{0,24},{8,16},{16,8},{24,0},{1,25},{9,17},{17,9},{25,1},{2,26},{10... | collective-permute-start | bytes 479240 | tf_op jit(solution)/shard_map/ppermute | solution.py:387
  21.8 3.9 %collective-permute-done.3 = bf16[208,384]{1,0:T(8,128)(2,1)S(1)} collective-permute-done((bf16[208,384]{1,0:T(8,128)(2,1)S(1)}, bf16[208,384]{1,0:T(8,128)(2,1)S(1)}, u32[]{:S(2)}, u32[]{:S(2)}) %collective-permute-start.3) | collective-permute-done | bytes 159776 | tf_op jit(solution)/shard_map/ppermute | solution.py:387
  25.7 14.8 %collective-permute-done.2 = bf16[208,384]{1,0:T(8,128)(2,1)S(1)} collective-permute-done((bf16[208,384]{1,0:T(8,128)(2,1)S(1)}, bf16[208,384]{1,0:T(8,128)(2,1)S(1)}, u32[]{:S(2)}, u32[]{:S(2)}) %collective-permute-start.2) | collective-permute-done | bytes 159776 | tf_op jit(solution)/shard_map/ppermute | solution.py:387
  40.7 1.6 collective-permute-start.6
  43.4 11.9 %collective-permute-done.8 = bf16[2,208,384]{2,1,0:T(8,128)(2,1)S(1)} collective-permute-done((bf16[2,208,384]{2,1,0:T(8,128)(2,1)S(1)}, bf16[2,208,384]{2,1,0:T(8,128)(2,1)S(1)}, u32[]{:S(2)}, u32[]{:S(2)}) %collective-permute-start.8) | collective-permute-done | bytes 319520 | tf_op jit(solution)/shard_map/ppermute | solution.py:383
  55.7 1.5 collective-permute-start.7
  57.2 1.0 fusion.28
  58.2 12.5 %collective-permute-done.9 = bf16[2,2,208,384]{3,2,0,1:T(8,128)(2,1)S(1)} collective-permute-done((bf16[2,2,208,384]{3,2,0,1:T(8,128)(2,1)S(1)}, bf16[2,2,208,384]{3,2,0,1:T(8,128)(2,1)S(1)}, u32[]{:S(2)}, u32[]{:S(2)}) %collective-permute-start.9) | collective-permute-done | bytes 639008 | tf_op jit(solution)/shard_map/ppermute | solution.py:379
  71.6 1.4 copy-done
  75.7 6.5 %enter_kernel.1 = (bf16[1024,768]{1,0:T(8,128)(2,1)}, bf16[1024,384]{1,0:T(8,128)(2,1)}, bf16[1024,384]{1,0:T(8,128)(2,1)}, bf16[1024,384]{1,0:T(8,128)(2,1)}) custom-call(s32[3]{0:T(128)} %pad_add_fusion.core_ref.place_ref, bf16[512,768]{1,0:T(8,128)(2,1)} %bitcast.254, bf16[512,768]{1,0:T(8,128)(2,1)} %copy-done.14, ...), custom_call_target="tpu_custom_call" | custom-call | bytes 1 | tf_op jit(solution)/shard_map/enter_kernel/pallas_call | solution.py:713
  82.1 21.0 %attend.1 = (bf16[1024,384]{1,0:T(8,128)(2,1)}, f32[3,2,1024]{2,1,0:T(2,128)}) custom-call(bf16[1024,384]{1,0:T(8,128)(2,1)} %get-tuple-element.114.q_ref, bf16[1024,384]{1,0:T(8,128)(2,1)} %get-tuple-element.115.k_ref, bf16[1024,384]{1,0:T(8,128)(2,1)} %get-tuple-element.116.v_ref), custom_call_target="tpu_custom_call" | custom-call | bytes 1 | tf_op jit(solution)/shard_map/attend/pallas_call | solution.py:526
  104.2 3.5 %out_kernel.1 = (f32[512,768]{1,0:T(8,128)}, bf16[512,768]{1,0:T(8,128)(2,1)}) custom-call(s32[3]{0:T(128)} %pad_add_fusion.core_ref.place_ref, bf16[1024,384]{1,0:T(8,128)(2,1)} %get-tuple-element.117.mixed_ref, bf16[384,768]{1,0:T(8,128)(2,1)} %bitcast.264), custom_call_target="tpu_custom_call" | custom-call | bytes 1 | tf_op jit(solution)/shard_map/out_kernel/pallas_call | solution.py:713
  108.3 2.5 collective-permute-done.11.received_ref
  111.7 3.0 %middle_kernel.1 = (f32[512,768]{1,0:T(8,128)}, bf16[512,768]{1,0:T(8,128)(2,1)}) custom-call(bf16[512,768]{1,0:T(8,128)(2,1)} %bitcast.255, f32[512,768]{1,0:T(8,128)} %get-tuple-element.118.part_ref, bf16[512,768]{1,0:T(8,128)(2,1)} %copy-done.21, f32[8,768]{1,0:T(8,128)} %convert_element_type.149.vec_ref), custom_call_target="tpu_custom_call" | custom-call | bytes 1 | tf_op jit(solution)/shard_map/middle_kernel/pallas_call | solution.py:735
  115.9 1.3 collective-permute-done.13.n_other
  118.2 22.4 %feed_forward.1 = (f32[512,768]{1,0:T(8,128)}, bf16[512,768]{1,0:T(8,128)(2,1)}, f32[512,768]{1,0:T(8,128)}, bf16[512,768]{1,0:T(8,128)(2,1)}, bf16[8,48,1536]{2...) custom-call(s32[3]{0:T(128)} %pad_add_fusion.core_ref.place_ref, ...), custom_call_target="tpu_custom_call" | custom-call | bytes 1 | tf_op jit(solution)/shard_map/feed_forward/pallas_call | solution.py:812
  141.0 1.1 collective-permute-start.15
  142.1 1.4 collective-permute-start.16
  144.4 4.2 %middle_back_kernel.1 = (f32[512,768]{1,0:T(8,128)}, bf16[512,768]{1,0:T(8,128)(2,1)}, f32[4,768]{1,0:T(4,128)}) custom-call(f32[512,768]{1,0:T(8,128)} %get-tuple-element.120.residual_ref, f32[512,768]{1,0:T(8,128)} %get-tuple-element.128.gn_ref, bf16[512,768]{1,0:T(8,128)(2,1)} %copy-done.17, bf16[512,768]{1,0:T(8,128)(2,1)} %bitcast.262, ...), custom_call_target="tpu_custom_call" | custom-call | bytes 1 | tf_op jit(solution)/shard_map/middle_back_kernel/pallas_call | solution.py:735
  148.6 2.5 collective-permute-done.18.other_ref
  152.0 4.4 %mixed_back_kernel.1 = (bf16[1024,384]{1,0:T(8,128)(2,1)}, bf16[384,768]{1,0:T(8,128)(2,1)}) custom-call(s32[3]{0:T(128)} %pad_add_fusion.core_ref.place_ref, bf16[1024,384]{1,0:T(8,128)(2,1)} %get-tuple-element.117.mixed_ref, bf16[512,768]{1,0:T(8,128)(2,1)} %get-tuple-element.130.mine_ref, bf16[512,768]{1,0:T(8,128)(2,1)} %copy-done.20, ...), custom_call_target="tpu_custom_call" | custom-call | bytes 1 | tf_op jit(solution)/shard_map/mixed_back_kernel/pallas_call | solution.py:713
  156.5 1.0 dynamic-slice_bitcast_fusion.2
  157.6 12.8 %attend_back.1 = (bf16[1024,384]{1,0:T(8,128)(2,1)}, bf16[1024,384]{1,0:T(8,128)(2,1)}, bf16[1024,384]{1,0:T(8,128)(2,1)}) custom-call(bf16[1024,384]{1,0:T(8,128)(2,1)} %get-tuple-element.114.q_ref, bf16[1024,384]{1,0:T(8,128)(2,1)} %get-tuple-element.115.k_ref, bf16[1024,384]{1,0:T(8,128)(2,1)} %get-tuple-element.116.v_ref, ...), custom_call_target="tpu_custom_call" | custom-call | bytes 1 | tf_op jit(solution)/shard_map/attend_back/pallas_call | solution.py:546
  170.5 1.1 copy-done.11
  174.5 1.3 collective-permute-start.20
  175.8 1.1 collective-permute-start.21
  180.7 5.6 %weight_back_kernel.1 = (bf16[8,96,384]{2,1,0:T(8,128)(2,1)}, bf16[8,96,384]{2,1,0:T(8,128)(2,1)}, bf16[4,2,48,384]{3,2,1,0:T(8,128)(2,1)}, bf16[4,2,48,384]{3,2,1,0:T(8,128)(2,1)}, f32[2,768]{1,0:T(2,128)}) custom-call(s32[3]{0:T(128)} %pad_add_fusion.core_ref.place_ref, bf16[1024,768]{1,0:T(8,128)(2,1)} %get-tuple-element.121.n_ref, ...), custom_call_target="tpu_custom_call" | custom-call | bytes 1 | tf_op jit(solution)/shard_map/weight_back_kernel/pallas_call | solution.py:713
  186.3 1.4 collective-permute-start.26
  187.7 1.0 collective-permute-start.25
  188.7 6.4 %enter_back_kernel.1 = (f32[512,768]{1,0:T(8,128)}, bf16[512,768]{1,0:T(8,128)(2,1)}) custom-call(s32[3]{0:T(128)} %pad_add_fusion.core_ref.place_ref, bf16[1024,384]{1,0:T(8,128)(2,1)} %get-tuple-element.154.q_ref, bf16[1024,384]{1,0:T(8,128)(2,1)} %get-tuple-element.155.k_ref, bf16[1024,384]{1,0:T(8,128)(2,1)} %get-tuple-element.156.v_ref, ...), custom_call_target="tpu_custom_call" | custom-call | bytes 1 | tf_op jit(solution)/shard_map/enter_back_kernel/pallas_call | solution.py:713
  195.1 2.2 collective-permute-done.23
  197.4 1.2 bitcast_add_fusion.1
  198.6 1.2 bitcast_add_fusion.2
  199.9 1.0 copy-done.44
  201.6 1.1 convert_add_fusion.3
  205.2 1.2 convert_add_fusion.2
  206.4 1.0 convert_add_fusion.4
  208.4 1.4 collective-permute-start.29
  210.6 4.3 %leave_kernel.1 = (f32[512,768]{1,0:T(8,128)}, f32[2,768]{1,0:T(2,128)}) custom-call(bf16[512,768]{1,0:T(8,128)(2,1)} %bitcast.256, f32[512,768]{1,0:T(8,128)} %get-tuple-element.161.gn_ref, bf16[512,768]{1,0:T(8,128)(2,1)} %copy-done.13, f32[512,768]{1,0:T(8,128)} %get-tuple-element.172.gr_ref, f32[8,768]{1,0:T(8,128)} %convert_element_type.149.vec_ref), custom_call_target="tpu_custom_call" | custom-call | bytes 1 | tf_op jit(solution)/shard_map/leave_kernel/pallas_call | solution.py:735
  214.9 1.2 fusion.5
  217.0 2.2 collective-permute-done.24
  219.2 1.2 bitcast_add_fusion
  220.5 2.2 collective-permute-start.34
  222.6 1.0 bitcast_add_fusion.5
  223.7 1.0 bitcast_add_fusion.6
  225.6 1.7 collective-permute-start.31
  227.3 1.2 collective-permute-start.32
  228.6 2.9 %collective-permute-done.32 = f32[10,768]{1,0:T(8,128)S(1)} collective-permute-done((f32[10,768]{1,0:T(8,128)S(1)}, f32[10,768]{1,0:T(8,128)S(1)}, u32[]{:S(2)}, u32[]{:S(2)}) %collective-permute-start.32) | collective-permute-done | bytes 30752 | tf_op jit(solution)/shard_map/ppermute | solution.py:383
  231.5 1.6 collective-permute-start.33
  233.9 1.8 collective-permute-done.33
  235.7 3.9 %collective-permute-done.31 = bf16[2,192,384]{2,1,0:T(8,128)(2,1)} collective-permute-done((bf16[2,192,384]{2,1,0:T(8,128)(2,1)}, bf16[2,192,384]{2,1,0:T(8,128)(2,1)}, u32[]{:S(2)}, u32[]{:S(2)}) %collective-permute-start.31) | collective-permute-done | bytes 294944 | tf_op jit(solution)/shard_map/ppermute | solution.py:387
  239.6 1.0 bitcast_add_fusion.4
  240.6 1.2 bitcast_add_fusion.3
  242.6 1.1 collective-permute-done.38
  243.7 1.3 collective-permute-start.39
  245.0 4.2 %collective-permute-done.39 = f32[10,768]{1,0:T(8,128)S(1)} collective-permute-done((f32[10,768]{1,0:T(8,128)S(1)}, f32[10,768]{1,0:T(8,128)S(1)}, u32[]{:S(2)}, u32[]{:S(2)}) %collective-permute-start.39) | collective-permute-done | bytes 30752 | tf_op jit(solution)/shard_map/ppermute | solution.py:387
  252.2 7.6 %collective-permute-done.35 = bf16[192,384]{1,0:T(8,128)(2,1)S(1)} collective-permute-done((bf16[192,384]{1,0:T(8,128)(2,1)S(1)}, bf16[192,384]{1,0:T(8,128)(2,1)S(1)}, u32[]{:S(2)}, u32[]{:S(2)}) %collective-permute-start.35) | collective-permute-done | bytes 147488 | tf_op jit(solution)/shard_map/ppermute | solution.py:387
  260.4 1.2 reshape.235
  262.3 1.3 fusion
  263.7 1.2 pad_maximum_fusion.2
  264.9 1.1 fusion.6
  (257 shorter events, 39.6 us)
Async XLA Ops:
  7.2 107.6 %all-gather.3.cloned.1.call-start = ((), (), s32[]{:S(2)}) async-start(), calls=%async_computation | async-start | bytes 5013504 | tf_op jit(solution)/shard_map/all_gather | solution.py:908
  9.7 2.1 copy-start.26
  9.8 1.4 collective-permute-start.12
  11.7 1.9 copy-start.18
  11.7 1.9 copy-start.19
  13.2 3.4 %collective-permute-start = (bf16[80,384]{1,0:T(8,128)(2,1)S(1)}, bf16[80,384]{1,0:T(8,128)(2,1)S(1)}, u32[]{:S(2)}, u32[]{:S(2)}) collective-permute-start(bf16[80,384]{1,0:T(8,128)(2,1)S(1)} %fusion.24), channel_id=1, source_target_pairs={{0,1},{1,0},{2,3},{3,2},{4,5},{5,4},{6,7},{7,6},{8,9},{9,8},{10,11... | collective-permute-start | bytes 184328 | tf_op jit(solution)/shard_map/ppermute | solution.py:375
  13.8 2.8 %copy-start.31 = (bf16[24,768]{1,0:T(8,128)(2,1)S(1)}, bf16[24,768]{1,0:T(8,128)(2,1)}, u32[]{:S(2)}) copy-start(bf16[24,768]{1,0:T(8,128)(2,1)} %param.24) | copy-start | bytes 110596
  13.9 26.7 %collective-permute-start.4 = (bf16[2,256,768]{2,1,0:T(8,128)(2,1)S(1)}, bf16[2,256,768]{2,1,0:T(8,128)(2,1)S(1)}, u32[]{:S(2)}, u32[]{:S(2)}) collective-permute-start(bf16[2,256,768]{2,1,0:T(8,128)(2,1)S(1)} %pad_maximum_fusion.6), channel_id=1, source_target_pairs={{0,2},{2,0},{1,3},{3,1},{4,6},{6,4},{5,7},{7,5},{8,10},{10,8},{9,1... | collective-permute-start | bytes 2359304 | tf_op jit(solution)/shard_map/ppermute | solution.py:383
  16.7 8.9 %collective-permute-start.3 = (bf16[208,384]{1,0:T(8,128)(2,1)S(1)}, bf16[208,384]{1,0:T(8,128)(2,1)S(1)}, u32[]{:S(2)}, u32[]{:S(2)}) collective-permute-start(bf16[208,384]{1,0:T(8,128)(2,1)S(1)} %pad_maximum_fusion.16), channel_id=1, source_target_pairs={{0,24},{8,16},{16,8},{24,0},{1,25},{9,17},{17,9},{25,1},{2,26},{10... | collective-permute-start | bytes 479240 | tf_op jit(solution)/shard_map/ppermute | solution.py:387
  20.4 20.1 %collective-permute-start.2 = (bf16[208,384]{1,0:T(8,128)(2,1)S(1)}, bf16[208,384]{1,0:T(8,128)(2,1)S(1)}, u32[]{:S(2)}, u32[]{:S(2)}) collective-permute-start(bf16[208,384]{1,0:T(8,128)(2,1)S(1)} %pad_maximum_fusion.16), channel_id=1, source_target_pairs={{0,16},{8,24},{16,0},{24,8},{1,17},{9,25},{17,1},{25,9},{2,18},{10... | collective-permute-start | bytes 479240 | tf_op jit(solution)/shard_map/ppermute | solution.py:387
  20.4 20.1 %collective-permute-start.1 = (bf16[208,384]{1,0:T(8,128)(2,1)S(1)}, bf16[208,384]{1,0:T(8,128)(2,1)S(1)}, u32[]{:S(2)}, u32[]{:S(2)}) collective-permute-start(bf16[208,384]{1,0:T(8,128)(2,1)S(1)} %pad_maximum_fusion.16), channel_id=1, source_target_pairs={{0,8},{8,0},{16,24},{24,16},{1,9},{9,1},{17,25},{25,17},{2,10},{10... | collective-permute-start | bytes 479240 | tf_op jit(solution)/shard_map/ppermute | solution.py:387
  40.7 14.9 %collective-permute-start.6 = (bf16[2,208,384]{2,1,0:T(8,128)(2,1)S(1)}, bf16[2,208,384]{2,1,0:T(8,128)(2,1)S(1)}, u32[]{:S(2)}, u32[]{:S(2)}) collective-permute-start(bf16[2,208,384]{2,1,0:T(8,128)(2,1)S(1)} %get-tuple-element.217), channel_id=1, source_target_pairs={{0,4},{4,0},{1,5},{5,1},{2,6},{6,2},{3,7},{7,3},{8,12},{12,8},{9,1... | collective-permute-start | bytes 958472 | tf_op jit(solution)/shard_map/ppermute | solution.py:379
  42.3 13.1 %collective-permute-start.8 = (bf16[2,208,384]{2,1,0:T(8,128)(2,1)S(1)}, bf16[2,208,384]{2,1,0:T(8,128)(2,1)S(1)}, u32[]{:S(2)}, u32[]{:S(2)}) collective-permute-start(bf16[2,208,384]{2,1,0:T(8,128)(2,1)S(1)} %get-tuple-element.218), channel_id=1, source_target_pairs={{0,2},{2,0},{1,3},{3,1},{4,6},{6,4},{5,7},{7,5},{8,10},{10,8},{9,1... | collective-permute-start | bytes 958472 | tf_op jit(solution)/shard_map/ppermute | solution.py:383
  55.5 15.2 %collective-permute-start.9 = (bf16[2,2,208,384]{3,2,0,1:T(8,128)(2,1)S(1)}, bf16[2,2,208,384]{3,2,0,1:T(8,128)(2,1)S(1)}, u32[]{:S(2)}, u32[]{:S(2)}) collective-permute-start(bf16[2,2,208,384]{3,2,0,1:T(8,128)(2,1)S(1)} %pad_maximum_fusion.10), channel_id=1, source_target_pairs={{0,4},{4,0},{1,5},{5,1},{2,6},{6,2},{3,7},{7,3},{8,12},{12,8},{9,1... | collective-permute-start | bytes 1916936 | tf_op jit(solution)/shard_map/ppermute | solution.py:379
  55.7 15.3 %collective-permute-start.7 = (bf16[2,2,208,384]{3,2,1,0:T(8,128)(2,1)S(1)}, bf16[2,2,208,384]{3,2,1,0:T(8,128)(2,1)S(1)}, u32[]{:S(2)}, u32[]{:S(2)}) collective-permute-start(bf16[2,2,208,384]{3,2,1,0:T(8,128)(2,1)S(1)} %pad_maximum_fusion.9), channel_id=1, source_target_pairs={{0,2},{2,0},{1,3},{3,1},{4,6},{6,4},{5,7},{7,5},{8,10},{10,8},{9,1... | collective-permute-start | bytes 1916936 | tf_op jit(solution)/shard_map/ppermute | solution.py:383
  58.2 12.6 %copy-start.1 = (bf16[1,2,256,768]{3,2,0,1:T(8,128)(2,1)}, bf16[1,2,256,768]{3,2,0,1:T(8,128)(2,1)S(1)}, u32[]{:S(2)}) copy-start(bf16[1,2,256,768]{3,2,0,1:T(8,128)(2,1)S(1)} %get-tuple-element.198) | copy-start | bytes 2359300
  58.2 16.6 %collective-permute-start.5 = (bf16[512,768]{1,0:T(8,128)(2,1)S(1)}, bf16[512,768]{1,0:T(8,128)(2,1)S(1)}, u32[]{:S(2)}, u32[]{:S(2)}) collective-permute-start(bf16[512,768]{1,0:T(8,128)(2,1)S(1)} %bitcast.253), channel_id=1, source_target_pairs={{0,1},{1,0},{2,3},{3,2},{4,5},{5,4},{6,7},{7,6},{8,9},{9,8},{10,11... | collective-permute-start | bytes 2359304 | tf_op jit(solution)/shard_map/ppermute | solution.py:375
  73.1 30.1 %collective-permute-start.10 = (bf16[8,24,768]{2,1,0:T(8,128)(2,1)S(1)}, bf16[8,24,768]{2,1,0:T(8,128)(2,1)S(1)}, u32[]{:S(2)}, u32[]{:S(2)}) collective-permute-start(bf16[8,24,768]{2,1,0:T(8,128)(2,1)S(1)} %dynamic-slice_bitcast_fusion.3), channel_id=1, source_target_pairs={{0,1},{1,0},{2,3},{3,2},{4,5},{5,4},{6,7},{7,6},{8,9},{9,8},{10,11... | collective-permute-start | bytes 884744 | tf_op jit(solution)/shard_map/ppermute | solution.py:375
  73.3 8.9 %copy-start.22 = (f32[32,8,24]{2,1,0:T(8,128)}, f32[32,8,24]{2,1,0:T(8,128)S(1)}, u32[]{:S(2)}) copy-start(f32[32,8,24]{2,1,0:T(8,128)S(1)} %reshape.240) | copy-start | bytes 73732
  103.3 5.0 %copy-start.4 = (bf16[1,2,256,768]{3,2,0,1:T(8,128)(2,1)S(1)}, bf16[1,2,256,768]{3,2,0,1:T(8,128)(2,1)}, u32[]{:S(2)}) copy-start(bf16[1,2,256,768]{3,2,0,1:T(8,128)(2,1)} %get-tuple-element.197) | copy-start | bytes 2359300
  107.7 3.2 %collective-permute-start.11 = (bf16[512,768]{1,0:T(8,128)(2,1)}, bf16[512,768]{1,0:T(8,128)(2,1)S(1)}, u32[]{:S(2)}, u32[]{:S(2)}) collective-permute-start(bf16[512,768]{1,0:T(8,128)(2,1)} %get-tuple-element.119), channel_id=1, source_target_pairs={{0,1},{1,0},{2,3},{3,2},{4,5},{5,4},{6,7},{7,6},{8,9},{9,8},{10,11... | collective-permute-start | bytes 2359304 | tf_op jit(solution)/shard_map/ppermute | solution.py:375
  108.3 7.7 %collective-permute-start.14 = (bf16[512,768]{1,0:T(8,128)(2,1)S(1)}, bf16[512,768]{1,0:T(8,128)(2,1)S(1)}, u32[]{:S(2)}, u32[]{:S(2)}) collective-permute-start(bf16[512,768]{1,0:T(8,128)(2,1)S(1)} %bitcast.263), channel_id=1, source_target_pairs={{0,1},{1,0},{2,3},{3,2},{4,5},{5,4},{6,7},{7,6},{8,9},{9,8},{10,11... | collective-permute-start | bytes 2359304 | tf_op jit(solution)/shard_map/ppermute | solution.py:375
  114.8 2.5 collective-permute-start.13
  140.6 2.9 %collective-permute-start.17 = (bf16[512,768]{1,0:T(8,128)(2,1)}, bf16[512,768]{1,0:T(8,128)(2,1)S(1)}, u32[]{:S(2)}, u32[]{:S(2)}) collective-permute-start(bf16[512,768]{1,0:T(8,128)(2,1)} %get-tuple-element.129), channel_id=1, source_target_pairs={{0,1},{1,0},{2,3},{3,2},{4,5},{5,4},{6,7},{7,6},{8,9},{9,8},{10,11... | collective-permute-start | bytes 2359304 | tf_op jit(solution)/shard_map/ppermute | solution.py:375
  141.0 29.5 %collective-permute-start.15 = (bf16[8,48,1536]{2,1,0:T(8,128)(2,1)}, bf16[8,48,1536]{2,1,0:T(8,128)(2,1)S(1)}, u32[]{:S(2)}, u32[]{:S(2)}) collective-permute-start(bf16[8,48,1536]{2,1,0:T(8,128)(2,1)} %get-tuple-element.126), channel_id=1, source_target_pairs={{0,2},{2,0},{1,3},{3,1},{4,6},{6,4},{5,7},{7,5},{8,10},{10,8},{9,1... | collective-permute-start | bytes 3538952 | tf_op jit(solution)/shard_map/ppermute | solution.py:383
  142.1 28.4 %collective-permute-start.16 = (bf16[4,2,96,768]{3,2,1,0:T(8,128)(2,1)}, bf16[4,2,96,768]{3,2,1,0:T(8,128)(2,1)S(1)}, u32[]{:S(2)}, u32[]{:S(2)}) collective-permute-start(bf16[4,2,96,768]{3,2,1,0:T(8,128)(2,1)} %get-tuple-element.127), channel_id=1, source_target_pairs={{0,4},{4,0},{1,5},{5,1},{2,6},{6,2},{3,7},{7,3},{8,12},{12,8},{9,1... | collective-permute-start | bytes 3538952 | tf_op jit(solution)/shard_map/ppermute | solution.py:379
  148.6 2.5 collective-permute-start.18
  157.4 19.5 %collective-permute-start.22 = (bf16[8,24,768]{2,1,0:T(8,128)(2,1)S(1)}, bf16[8,24,768]{2,1,0:T(8,128)(2,1)S(1)}, u32[]{:S(2)}, u32[]{:S(2)}) collective-permute-start(bf16[8,24,768]{2,1,0:T(8,128)(2,1)S(1)} %dynamic-slice_bitcast_fusion.2), channel_id=1, source_target_pairs={{0,1},{1,0},{2,3},{3,2},{4,5},{5,4},{6,7},{7,6},{8,9},{9,8},{10,11... | collective-permute-start | bytes 884744 | tf_op jit(solution)/shard_map/ppermute | solution.py:375
  157.6 14.0 %copy-start.10 = (bf16[8,48,1536]{2,1,0:T(8,128)(2,1)S(1)}, bf16[8,48,1536]{2,1,0:T(8,128)(2,1)}, u32[]{:S(2)}) copy-start(bf16[8,48,1536]{2,1,0:T(8,128)(2,1)} %get-tuple-element.125) | copy-start | bytes 3538948
  171.6 1.6 copy-start.12
  173.5 3.5 %copy-start.2 = (f32[4,2,96,768]{3,2,1,0:T(8,128)}, f32[4,2,96,768]{3,2,1,0:T(8,128)S(1)}, u32[]{:S(2)}) copy-start(f32[4,2,96,768]{3,2,1,0:T(8,128)S(1)} %convert_add_fusion) | copy-start | bytes 7077892
  173.5 3.4 %copy-start.24 = (bf16[384,768]{1,0:T(8,128)(2,1)S(1)}, bf16[384,768]{1,0:T(8,128)(2,1)}, u32[]{:S(2)}) copy-start(bf16[384,768]{1,0:T(8,128)(2,1)} %get-tuple-element.153) | copy-start | bytes 1769476
  174.5 22.8 %collective-permute-start.20 = (bf16[4,48,1536]{2,1,0:T(8,128)(2,1)}, bf16[4,48,1536]{2,1,0:T(8,128)(2,1)}, u32[]{:S(2)}, u32[]{:S(2)}) collective-permute-start(bf16[4,48,1536]{2,1,0:T(8,128)(2,1)} %fusion.3), channel_id=1, source_target_pairs={{0,4},{4,0},{1,5},{5,1},{2,6},{6,2},{3,7},{7,3},{8,12},{12,8},{9,1... | collective-permute-start | bytes 1769480 | tf_op jit(solution)/shard_map/ppermute | solution.py:379
  175.8 21.5 %collective-permute-start.21 = (bf16[4,96,768]{2,1,0:T(8,128)(2,1)S(1)}, bf16[4,96,768]{2,1,0:T(8,128)(2,1)}, u32[]{:S(2)}, u32[]{:S(2)}) collective-permute-start(bf16[4,96,768]{2,1,0:T(8,128)(2,1)S(1)} %fusion.2), channel_id=1, source_target_pairs={{0,2},{2,0},{1,3},{3,1},{4,6},{6,4},{5,7},{7,5},{8,10},{10,8},{9,1... | collective-permute-start | bytes 1769480 | tf_op jit(solution)/shard_map/ppermute | solution.py:383
  177.8 19.6 %collective-permute-start.23 = (bf16[4,2,24,768]{3,2,1,0:T(8,128)(2,1)}, bf16[4,2,24,768]{3,2,1,0:T(8,128)(2,1)}, u32[]{:S(2)}, u32[]{:S(2)}) collective-permute-start(bf16[4,2,24,768]{3,2,1,0:T(8,128)(2,1)} %dynamic-slice_bitcast_fusion.1), channel_id=1, source_target_pairs={{0,4},{4,0},{1,5},{5,1},{2,6},{6,2},{3,7},{7,3},{8,12},{12,8},{9,1... | collective-permute-start | bytes 884744 | tf_op jit(solution)/shard_map/ppermute | solution.py:379
  186.3 11.0 %copy-start.3 = (f32[4,2,96,768]{3,2,1,0:T(8,128)S(1)}, f32[4,2,96,768]{3,2,1,0:T(8,128)}, u32[]{:S(2)}) copy-start(f32[4,2,96,768]{3,2,1,0:T(8,128)} %copy-done.2) | copy-start | bytes 7077892
  186.3 18.4 %collective-permute-start.26 = (bf16[4,2,48,384]{3,2,1,0:T(8,128)(2,1)}, bf16[4,2,48,384]{3,2,1,0:T(8,128)(2,1)}, u32[]{:S(2)}, u32[]{:S(2)}) collective-permute-start(bf16[4,2,48,384]{3,2,1,0:T(8,128)(2,1)} %get-tuple-element.164), channel_id=1, source_target_pairs={{0,4},{4,0},{1,5},{5,1},{2,6},{6,2},{3,7},{7,3},{8,12},{12,8},{9,1... | collective-permute-start | bytes 884744 | tf_op jit(solution)/shard_map/ppermute | solution.py:379
  187.7 17.0 %collective-permute-start.25 = (bf16[8,96,384]{2,1,0:T(8,128)(2,1)}, bf16[8,96,384]{2,1,0:T(8,128)(2,1)}, u32[]{:S(2)}, u32[]{:S(2)}) collective-permute-start(bf16[8,96,384]{2,1,0:T(8,128)(2,1)} %get-tuple-element.163), channel_id=1, source_target_pairs={{0,2},{2,0},{1,3},{3,1},{4,6},{6,4},{5,7},{7,5},{8,10},{10,8},{9,1... | collective-permute-start | bytes 1769480 | tf_op jit(solution)/shard_map/ppermute | solution.py:383
  197.3 6.8 %collective-permute-start.19 = (bf16[512,768]{1,0:T(8,128)(2,1)}, bf16[512,768]{1,0:T(8,128)(2,1)S(1)}, u32[]{:S(2)}, u32[]{:S(2)}) collective-permute-start(bf16[512,768]{1,0:T(8,128)(2,1)} %get-tuple-element.150), channel_id=1, source_target_pairs={{0,1},{1,0},{2,3},{3,2},{4,5},{5,4},{6,7},{7,6},{8,9},{9,8},{10,11... | collective-permute-start | bytes 2359304 | tf_op jit(solution)/shard_map/ppermute | solution.py:375
  200.9 3.9 %collective-permute-start.27 = (bf16[512,768]{1,0:T(8,128)(2,1)S(1)}, bf16[512,768]{1,0:T(8,128)(2,1)S(1)}, u32[]{:S(2)}, u32[]{:S(2)}) collective-permute-start(bf16[512,768]{1,0:T(8,128)(2,1)S(1)} %copy-done.44), channel_id=1, source_target_pairs={{0,1},{1,0},{2,3},{3,2},{4,5},{5,4},{6,7},{7,6},{8,9},{9,8},{10,11... | collective-permute-start | bytes 2359304 | tf_op jit(solution)/shard_map/ppermute | solution.py:375
  201.6 2.5 copy-start.8
  202.7 1.7 copy-start.5
  202.7 1.7 copy-start.34
  203.6 15.6 %collective-permute-start.24 = (bf16[2,192,768]{2,1,0:T(8,128)(2,1)}, bf16[2,192,768]{2,1,0:T(8,128)(2,1)}, u32[]{:S(2)}, u32[]{:S(2)}) collective-permute-start(bf16[2,192,768]{2,1,0:T(8,128)(2,1)} %fusion.4), channel_id=1, source_target_pairs={{0,8},{8,0},{16,24},{24,16},{1,9},{9,1},{17,25},{25,17},{2,10},{10... | collective-permute-start | bytes 1769480 | tf_op jit(solution)/shard_map/ppermute | solution.py:387
  204.7 1.7 copy-start.25
  204.8 1.6 copy-start.13
  208.4 14.3 %collective-permute-start.29 = (bf16[4,96,384]{2,1,0:T(8,128)(2,1)S(1)}, bf16[4,96,384]{2,1,0:T(8,128)(2,1)}, u32[]{:S(2)}, u32[]{:S(2)}) collective-permute-start(bf16[4,96,384]{2,1,0:T(8,128)(2,1)S(1)} %fusion.12), channel_id=1, source_target_pairs={{0,4},{4,0},{1,5},{5,1},{2,6},{6,2},{3,7},{7,3},{8,12},{12,8},{9,1... | collective-permute-start | bytes 884744 | tf_op jit(solution)/shard_map/ppermute | solution.py:379
  209.8 12.8 %collective-permute-start.30 = (bf16[4,96,384]{2,1,0:T(8,128)(2,1)}, bf16[4,96,384]{2,1,0:T(8,128)(2,1)}, u32[]{:S(2)}, u32[]{:S(2)}) collective-permute-start(bf16[4,96,384]{2,1,0:T(8,128)(2,1)} %fusion.10), channel_id=1, source_target_pairs={{0,2},{2,0},{1,3},{3,1},{4,6},{6,4},{5,7},{7,5},{8,10},{10,8},{9,1... | collective-permute-start | bytes 884744 | tf_op jit(solution)/shard_map/ppermute | solution.py:383
  220.5 19.1 %collective-permute-start.34 = (bf16[192,768]{1,0:T(8,128)(2,1)S(1)}, bf16[192,768]{1,0:T(8,128)(2,1)}, u32[]{:S(2)}, u32[]{:S(2)}) collective-permute-start(bf16[192,768]{1,0:T(8,128)(2,1)S(1)} %fusion.11), channel_id=1, source_target_pairs={{0,16},{8,24},{16,0},{24,8},{1,17},{9,25},{17,1},{25,9},{2,18},{10... | collective-permute-start | bytes 884744 | tf_op jit(solution)/shard_map/ppermute | solution.py:387
  224.7 2.6 copy-start.27
  224.7 2.6 copy-start.32
  224.7 2.6 copy-start.33
  225.6 14.0 %collective-permute-start.31 = (bf16[2,192,384]{2,1,0:T(8,128)(2,1)}, bf16[2,192,384]{2,1,0:T(8,128)(2,1)}, u32[]{:S(2)}, u32[]{:S(2)}) collective-permute-start(bf16[2,192,384]{2,1,0:T(8,128)(2,1)} %fusion.13), channel_id=1, source_target_pairs={{0,8},{8,0},{16,24},{24,16},{1,9},{9,1},{17,25},{25,17},{2,10},{10... | collective-permute-start | bytes 884744 | tf_op jit(solution)/shard_map/ppermute | solution.py:387
  227.3 4.2 %collective-permute-start.32 = (f32[10,768]{1,0:T(8,128)S(1)}, f32[10,768]{1,0:T(8,128)S(1)}, u32[]{:S(2)}, u32[]{:S(2)}) collective-permute-start(f32[10,768]{1,0:T(8,128)S(1)} %pad_maximum_fusion.22), channel_id=1, source_target_pairs={{0,2},{2,0},{1,3},{3,1},{4,6},{6,4},{5,7},{7,5},{8,10},{10,8},{9,1... | collective-permute-start | bytes 92168 | tf_op jit(solution)/shard_map/ppermute | solution.py:383
  231.5 4.2 %collective-permute-start.33 = (f32[10,768]{1,0:T(8,128)S(1)}, f32[10,768]{1,0:T(8,128)S(1)}, u32[]{:S(2)}, u32[]{:S(2)}) collective-permute-start(f32[10,768]{1,0:T(8,128)S(1)} %fusion.27), channel_id=1, source_target_pairs={{0,4},{4,0},{1,5},{5,1},{2,6},{6,2},{3,7},{7,3},{8,12},{12,8},{9,1... | collective-permute-start | bytes 92168 | tf_op jit(solution)/shard_map/ppermute | solution.py:379
  233.1 29.2 %collective-permute-start.28 = (bf16[512,768]{1,0:T(8,128)(2,1)}, bf16[512,768]{1,0:T(8,128)(2,1)}, u32[]{:S(2)}, u32[]{:S(2)}) collective-permute-start(bf16[512,768]{1,0:T(8,128)(2,1)} %pad_maximum_fusion.7), channel_id=1, source_target_pairs={{0,2},{2,0},{1,3},{3,1},{4,6},{6,4},{5,7},{7,5},{8,10},{10,8},{9,1... | collective-permute-start | bytes 2359304 | tf_op jit(solution)/shard_map/ppermute | solution.py:383
  239.6 4.1 %collective-permute-start.38 = (f32[10,768]{1,0:T(8,128)S(1)}, f32[10,768]{1,0:T(8,128)S(1)}, u32[]{:S(2)}, u32[]{:S(2)}) collective-permute-start(f32[10,768]{1,0:T(8,128)S(1)} %add.195), channel_id=1, source_target_pairs={{0,8},{8,0},{16,24},{24,16},{1,9},{9,1},{17,25},{25,17},{2,10},{10... | collective-permute-start | bytes 92168 | tf_op jit(solution)/shard_map/ppermute | solution.py:387
  240.6 4.4 %copy-start.6 = (f32[2,192,384]{2,1,0:T(8,128)}, f32[2,192,384]{2,1,0:T(8,128)S(1)}, u32[]{:S(2)}) copy-start(f32[2,192,384]{2,1,0:T(8,128)S(1)} %bitcast_add_fusion.4) | copy-start | bytes 1769476
  243.7 5.6 %collective-permute-start.39 = (f32[10,768]{1,0:T(8,128)S(1)}, f32[10,768]{1,0:T(8,128)S(1)}, u32[]{:S(2)}, u32[]{:S(2)}) collective-permute-start(f32[10,768]{1,0:T(8,128)S(1)} %add.202), channel_id=1, source_target_pairs={{0,16},{8,24},{16,0},{24,8},{1,17},{9,25},{17,1},{25,9},{2,18},{10... | collective-permute-start | bytes 92168 | tf_op jit(solution)/shard_map/ppermute | solution.py:387
  245.0 14.7 %copy-start.7 = (f32[2,192,384]{2,1,0:T(8,128)S(1)}, f32[2,192,384]{2,1,0:T(8,128)}, u32[]{:S(2)}) copy-start(f32[2,192,384]{2,1,0:T(8,128)} %copy-done.6) | copy-start | bytes 1769476
  249.3 2.1 collective-permute-start.40
  249.4 2.6 collective-permute-start.37
  249.9 9.9 %collective-permute-start.35 = (bf16[192,384]{1,0:T(8,128)(2,1)S(1)}, bf16[192,384]{1,0:T(8,128)(2,1)S(1)}, u32[]{:S(2)}, u32[]{:S(2)}) collective-permute-start(bf16[192,384]{1,0:T(8,128)(2,1)S(1)} %fusion.18), channel_id=1, source_target_pairs={{0,16},{8,24},{16,0},{24,8},{1,17},{9,25},{17,1},{25,9},{2,18},{10... | collective-permute-start | bytes 442376 | tf_op jit(solution)/shard_map/ppermute | solution.py:387
  259.9 7.1 %collective-permute-start.36 = (f32[3,24,384]{2,1,0:T(8,128)S(1)}, f32[3,24,384]{2,1,0:T(8,128)S(1)}, u32[]{:S(2)}, u32[]{:S(2)}) collective-permute-start(f32[3,24,384]{2,1,0:T(8,128)S(1)} %dynamic-slice_bitcast_fusion.5), channel_id=1, source_target_pairs={{0,1},{1,0},{2,3},{3,2},{4,5},{5,4},{6,7},{7,6},{8,9},{9,8},{10,11... | collective-permute-start | bytes 331784 | tf_op jit(solution)/shard_map/ppermute | solution.py:375
  (23 other events, 27.2 us)
Sparse Core Ops, SparseCore 0:
  12.7 92.1 all-gather.2
where the time goes:
time: 278 us; the launch traced here: 276 us
  Pallas kernels  94.3 us (34%)
  waiting for transfers between devices  76.1 us (27%)
  starting transfers between devices  35.4 us (13%)
  local copies, waits for them, and re-layouts  30.8 us (11%)
  other arithmetic  24 us (9%)
  between operations  15.7 us (6%)
    ppermute x9, waiting for transfers between devices, other_z(): lax.ppermute(value, 'z', [(i, i ^ by) for i in range(lax.axis_size('z'))])  37.7 us
    pallas_call x5, Pallas kernels, whole_call(): pl.pallas_call(kernel, in_specs=in_specs, out_specs=[pl.BlockSpec(memory_...  26.5 us
    pallas_call x1, Pallas kernels, feed_forward(): pl.pallas_call(hidden_kernel, grid=(steps,), in_specs=[pl.BlockSpec(memor...  22.4 us
    pallas_call x1, Pallas kernels, attend(): pl.pallas_call(attend_kernel, grid=(pairs,), in_specs=[block] * 3, out_sp...  21 us
    ppermute x8, waiting for transfers between devices, other_x(): return lax.ppermute(value, 'x', [(0, 1), (1, 0)])  16.4 us
    ppermute x9, waiting for transfers between devices, other_y(): return lax.ppermute(value, 'y', [(0, 1), (1, 0)])  14.9 us
    pallas_call x1, Pallas kernels, attend_back(): pl.pallas_call(attend_back_kernel, grid=(pairs,), in_specs=[block] * 5 +...  12.8 us
    add x13, other arithmetic, plus(): return kept.astype(F32) + received.astype(F32)  11.8 us
  transfers between devices with their start and end apart: 42, of which 16 were waited for; matrix products, arithmetic and copies ran while one was open for 14% of the time, Pallas kernels for 26%

commit v1 on v0

--- a/solution.py
+++ b/solution.py
@@ -1043,35 +1043,43 @@
 
     left_from, right_from, sums1 = lax.optimization_barrier((left_from, right_from, sums1))
     small_grads = jnp.concatenate((sums_heads, sums2, sums1, up_sums.reshape(2, width)))
+    lefts = plus(pick(lefts, x, 1), left_from)
+    rights = plus(pick(rights, y, 1), right_from)
+    last = jnp.concatenate((lefts, rights), axis=1)
+    last, small_grads = lax.optimization_barrier((last, small_grads))
+    last, last_from = first_z(last)
     small_grads = small_grads + other_y(small_grads)
     small_grads = small_grads + other_x(small_grads)
-    lefts = plus(pick(lefts, x, 1), left_from)
-    rights = plus(pick(rights, y, 1), right_from)
-    last, last_from = first_z(jnp.concatenate((lefts, rights), axis=1))
-    last_from, small_grads = lax.optimization_barrier((last_from, small_grads))
-    small_grads = small_grads + other_z(small_grads, 1)
-    small_grads = small_grads + other_z(small_grads, 2)
-    small_core = small_grads[:8] + other_core(small_grads[:8])
-    last_from, forward_from = lax.optimization_barrier((last_from, forward_from))
+    small_from = other_z(small_grads, 1)
+    last_from, small_from, from_y, forward_from = lax.optimization_barrier(
+        (last_from, small_from, from_y, forward_from)
+    )
     last, last_from = second_z(plus(last, last_from))
+    small_grads = small_grads + small_from
+    small_from = other_z(small_grads, 2)
     forward_sum = plus(forward_kept, forward_from)
-    last = plus(last, last_from)
     layer_out = pair(y, pick(output, y, 0), from_y[:block])
     grad_tokens = pair(y, pick(grad_tokens, y, 0), from_y[block:].astype(F32))
 
     up_mine = forward_sum[: 4 * rows].reshape(2, 2, rows, width)
     down_mine = forward_sum[4 * rows :]
+    up_from = other_core(pick(up_mine, 1 - core, 1))
+    up_out = pair(core, pick(up_mine, core, 1), up_from)
+    up_out = up_out.reshape(2, 2, rows, half_chips, hidden_rows)
+    up_out = jnp.transpose(up_out, (2, 1, 3, 0, 4)).reshape(rows, 2 * hidden)
+    last_from, small_from, layer_out, grad_tokens, up_out, down_mine = lax.optimization_barrier(
+        (last_from, small_from, layer_out, grad_tokens, up_out, down_mine)
+    )
+    last = plus(last, last_from)
+    small_grads = small_grads + small_from
+    small_core = small_grads[:8] + other_core(small_grads[:8])
     three_mine = last[: 6 * rows].reshape(3, 2, rows, half)
+    three_from = other_core(pick(three_mine, 1 - core, 1))
     out_mine = jnp.concatenate((last[6 * rows : 7 * rows], last[7 * rows : 8 * rows]), axis=1)
-    up_from = other_core(pick(up_mine, 1 - core, 1))
     chip = (z * 2 + x) * 2 + y
     small_mine = lax.dynamic_slice_in_dim(small_core, (chip * 2 + core) * rows, rows, 1)
     up_bias = lax.dynamic_slice_in_dim(small_grads[8:].reshape(hidden), chip * hidden_rows, hidden_rows, 0)
-    three_from = other_core(pick(three_mine, 1 - core, 1))
     three_out = pair(core, pick(three_mine, core, 1), three_from)
-    up_out = pair(core, pick(up_mine, core, 1), up_from)
-    up_out = up_out.reshape(2, 2, rows, half_chips, hidden_rows)
-    up_out = jnp.transpose(up_out, (2, 1, 3, 0, 4)).reshape(rows, 2 * hidden)
     g_q, g_k, g_v = (jnp.concatenate((three_out[0, i], three_out[1, i]), axis=1) for i in range(3))
     g_small = [small_mine[i] for i in (0, 1, 2, 3, 6, 7, 4, 5)]
     return (

time: 278 us -> 282 us (1.014)
    ppermute x9, waiting for transfers between devices: 14.9 us -> 25.1 us  [other_y(): return lax.ppermute(value, 'y', [(0, 1), (1, 0)])]
    ppermute x9, waiting for transfers between devices: 37.7 us -> 28.2 us  [other_z(): lax.ppermute(value, 'z', [(i, i ^ by) for i in range(lax.axis_size('z'))])]
    unnamed x98 -> x94, local copies, waits for them, and re-layouts: 11.6 us -> 11.6 us
  transfers between devices with their start and end apart: 42 -> 42, of which waited for: 16 -> 14; matrix products, arithmetic and copies ran while one was open for 14% -> 12% of each run, Pallas kernels for 26% -> 26%
where the time goes in v1:
time: 282 us; the launch traced here: 280 us
  Pallas kernels  94.2 us (33%)
  waiting for transfers between devices  77.7 us (28%)
  starting transfers between devices  37.7 us (13%)
  local copies, waits for them, and re-layouts  30.7 us (11%)
  other arithmetic  23.7 us (8%)
  between operations  15.7 us (6%)
    ppermute x9, waiting for transfers between devices, other_z(): lax.ppermute(value, 'z', [(i, i ^ by) for i in range(lax.axis_size('z'))])  28.2 us
    pallas_call x5, Pallas kernels, whole_call(): pl.pallas_call(kernel, in_specs=in_specs, out_specs=[pl.BlockSpec(memory_...  26.5 us
    ppermute x9, waiting for transfers between devices, other_y(): return lax.ppermute(value, 'y', [(0, 1), (1, 0)])  25.1 us
    pallas_call x1, Pallas kernels, feed_forward(): pl.pallas_call(hidden_kernel, grid=(steps,), in_specs=[pl.BlockSpec(memor...  22.4 us
    pallas_call x1, Pallas kernels, attend(): pl.pallas_call(attend_kernel, grid=(pairs,), in_specs=[block] * 3, out_sp...  21 us
    ppermute x8, waiting for transfers between devices, other_x(): return lax.ppermute(value, 'x', [(0, 1), (1, 0)])  17.2 us
    ppermute x9, starting transfers between devices, other_z(): lax.ppermute(value, 'z', [(i, i ^ by) for i in range(lax.axis_size('z'))])  13.2 us
    pallas_call x1, Pallas kernels, attend_back(): pl.pallas_call(attend_back_kernel, grid=(pairs,), in_specs=[block] * 5 +...  12.8 us
  transfers between devices with their start and end apart: 42, of which 14 were waited for; matrix products, arithmetic and copies ran while one was open for 12% of the time, Pallas kernels for 26%

profile of v1, /device:TPU:0, one launch (start us, length us, event | category | flops | bytes accessed | tf_op | source)
XLA Modules:
  0.0 279.8 jit_solution(16679822996260487344)
XLA Ops:
  7.2 1.1 reshape.217
  8.4 1.3 dynamic-slice_reduce_fusion.1
  13.9 2.7 collective-permute-start.4
  16.7 3.7 %collective-permute-start.3 = (bf16[208,384]{1,0:T(8,128)(2,1)S(1)}, bf16[208,384]{1,0:T(8,128)(2,1)S(1)}, u32[]{:S(2)}, u32[]{:S(2)}) collective-permute-start(bf16[208,384]{1,0:T(8,128)(2,1)S(1)} %pad_maximum_fusion.16), channel_id=1, source_target_pairs={{0,24},{8,16},{16,8},{24,0},{1,25},{9,17},{17,9},{25,1},{2,26},{10... | collective-permute-start | bytes 479240 | tf_op jit(solution)/shard_map/ppermute | solution.py:387
  21.8 3.9 %collective-permute-done.3 = bf16[208,384]{1,0:T(8,128)(2,1)S(1)} collective-permute-done((bf16[208,384]{1,0:T(8,128)(2,1)S(1)}, bf16[208,384]{1,0:T(8,128)(2,1)S(1)}, u32[]{:S(2)}, u32[]{:S(2)}) %collective-permute-start.3) | collective-permute-done | bytes 159776 | tf_op jit(solution)/shard_map/ppermute | solution.py:387
  25.7 14.8 %collective-permute-done.2 = bf16[208,384]{1,0:T(8,128)(2,1)S(1)} collective-permute-done((bf16[208,384]{1,0:T(8,128)(2,1)S(1)}, bf16[208,384]{1,0:T(8,128)(2,1)S(1)}, u32[]{:S(2)}, u32[]{:S(2)}) %collective-permute-start.2) | collective-permute-done | bytes 159776 | tf_op jit(solution)/shard_map/ppermute | solution.py:387
  40.7 1.6 collective-permute-start.6
  43.4 11.9 %collective-permute-done.8 = bf16[2,208,384]{2,1,0:T(8,128)(2,1)S(1)} collective-permute-done((bf16[2,208,384]{2,1,0:T(8,128)(2,1)S(1)}, bf16[2,208,384]{2,1,0:T(8,128)(2,1)S(1)}, u32[]{:S(2)}, u32[]{:S(2)}) %collective-permute-start.8) | collective-permute-done | bytes 319520 | tf_op jit(solution)/shard_map/ppermute | solution.py:383
  55.7 1.5 collective-permute-start.7
  57.2 1.0 fusion.27
  58.2 12.5 %collective-permute-done.9 = bf16[2,2,208,384]{3,2,0,1:T(8,128)(2,1)S(1)} collective-permute-done((bf16[2,2,208,384]{3,2,0,1:T(8,128)(2,1)S(1)}, bf16[2,2,208,384]{3,2,0,1:T(8,128)(2,1)S(1)}, u32[]{:S(2)}, u32[]{:S(2)}) %collective-permute-start.9) | collective-permute-done | bytes 639008 | tf_op jit(solution)/shard_map/ppermute | solution.py:379
  71.6 1.4 copy-done
  75.7 6.5 %enter_kernel.1 = (bf16[1024,768]{1,0:T(8,128)(2,1)}, bf16[1024,384]{1,0:T(8,128)(2,1)}, bf16[1024,384]{1,0:T(8,128)(2,1)}, bf16[1024,384]{1,0:T(8,128)(2,1)}) custom-call(s32[3]{0:T(128)} %pad_add_fusion.core_ref.place_ref, bf16[512,768]{1,0:T(8,128)(2,1)} %bitcast.254, bf16[512,768]{1,0:T(8,128)(2,1)} %copy-done.12, ...), custom_call_target="tpu_custom_call" | custom-call | bytes 1 | tf_op jit(solution)/shard_map/enter_kernel/pallas_call | solution.py:713
  82.1 21.0 %attend.1 = (bf16[1024,384]{1,0:T(8,128)(2,1)}, f32[3,2,1024]{2,1,0:T(2,128)}) custom-call(bf16[1024,384]{1,0:T(8,128)(2,1)} %get-tuple-element.123.q_ref, bf16[1024,384]{1,0:T(8,128)(2,1)} %get-tuple-element.124.k_ref, bf16[1024,384]{1,0:T(8,128)(2,1)} %get-tuple-element.125.v_ref), custom_call_target="tpu_custom_call" | custom-call | bytes 1 | tf_op jit(solution)/shard_map/attend/pallas_call | solution.py:526
  104.1 3.6 %out_kernel.1 = (f32[512,768]{1,0:T(8,128)}, bf16[512,768]{1,0:T(8,128)(2,1)}) custom-call(s32[3]{0:T(128)} %pad_add_fusion.core_ref.place_ref, bf16[1024,384]{1,0:T(8,128)(2,1)} %get-tuple-element.126.mixed_ref, bf16[384,768]{1,0:T(8,128)(2,1)} %bitcast.264), custom_call_target="tpu_custom_call" | custom-call | bytes 1 | tf_op jit(solution)/shard_map/out_kernel/pallas_call | solution.py:713
  108.3 2.5 collective-permute-done.12.received_ref
  111.8 3.0 %middle_kernel.1 = (f32[512,768]{1,0:T(8,128)}, bf16[512,768]{1,0:T(8,128)(2,1)}) custom-call(bf16[512,768]{1,0:T(8,128)(2,1)} %bitcast.255, f32[512,768]{1,0:T(8,128)} %get-tuple-element.127.part_ref, bf16[512,768]{1,0:T(8,128)(2,1)} %copy-done.19, f32[8,768]{1,0:T(8,128)} %convert_element_type.149.vec_ref), custom_call_target="tpu_custom_call" | custom-call | bytes 1 | tf_op jit(solution)/shard_map/middle_kernel/pallas_call | solution.py:735
  115.9 1.3 collective-permute-done.13.n_other
  118.2 22.4 %feed_forward.1 = (f32[512,768]{1,0:T(8,128)}, bf16[512,768]{1,0:T(8,128)(2,1)}, f32[512,768]{1,0:T(8,128)}, bf16[512,768]{1,0:T(8,128)(2,1)}, bf16[8,48,1536]{2...) custom-call(s32[3]{0:T(128)} %pad_add_fusion.core_ref.place_ref, ...), custom_call_target="tpu_custom_call" | custom-call | bytes 1 | tf_op jit(solution)/shard_map/feed_forward/pallas_call | solution.py:812
  141.0 1.1 collective-permute-start.15
  142.1 1.4 collective-permute-start.16
  144.4 4.2 %middle_back_kernel.1 = (f32[512,768]{1,0:T(8,128)}, bf16[512,768]{1,0:T(8,128)(2,1)}, f32[4,768]{1,0:T(4,128)}) custom-call(f32[512,768]{1,0:T(8,128)} %get-tuple-element.135.residual_ref, f32[512,768]{1,0:T(8,128)} %get-tuple-element.136.gn_ref, bf16[512,768]{1,0:T(8,128)(2,1)} %copy-done.15, bf16[512,768]{1,0:T(8,128)(2,1)} %bitcast.262, ...), custom_call_target="tpu_custom_call" | custom-call | bytes 1 | tf_op jit(solution)/shard_map/middle_back_kernel/pallas_call | solution.py:735
  148.7 2.5 collective-permute-done.18.other_ref
  152.0 4.4 %mixed_back_kernel.1 = (bf16[1024,384]{1,0:T(8,128)(2,1)}, bf16[384,768]{1,0:T(8,128)(2,1)}) custom-call(s32[3]{0:T(128)} %pad_add_fusion.core_ref.place_ref, bf16[1024,384]{1,0:T(8,128)(2,1)} %get-tuple-element.126.mixed_ref, bf16[512,768]{1,0:T(8,128)(2,1)} %get-tuple-element.138.mine_ref, bf16[512,768]{1,0:T(8,128)(2,1)} %copy-done.18, ...), custom_call_target="tpu_custom_call" | custom-call | bytes 1 | tf_op jit(solution)/shard_map/mixed_back_kernel/pallas_call | solution.py:713
  156.4 1.0 dynamic-slice_bitcast_fusion.2
  157.6 12.8 %attend_back.1 = (bf16[1024,384]{1,0:T(8,128)(2,1)}, bf16[1024,384]{1,0:T(8,128)(2,1)}, bf16[1024,384]{1,0:T(8,128)(2,1)}) custom-call(bf16[1024,384]{1,0:T(8,128)(2,1)} %get-tuple-element.123.q_ref, bf16[1024,384]{1,0:T(8,128)(2,1)} %get-tuple-element.124.k_ref, bf16[1024,384]{1,0:T(8,128)(2,1)} %get-tuple-element.125.v_ref, ...), custom_call_target="tpu_custom_call" | custom-call | bytes 1 | tf_op jit(solution)/shard_map/attend_back/pallas_call | solution.py:546
  170.5 1.1 copy-done.9
  174.5 1.3 collective-permute-start.21
  175.8 1.1 collective-permute-start.22
  178.4 1.0 slice_reduce_fusion
  180.7 5.6 %weight_back_kernel.1 = (bf16[8,96,384]{2,1,0:T(8,128)(2,1)}, bf16[8,96,384]{2,1,0:T(8,128)(2,1)}, bf16[4,2,48,384]{3,2,1,0:T(8,128)(2,1)}, bf16[4,2,48,384]{3,2,1,0:T(8,128)(2,1)}, f32[2,768]{1,0:T(2,128)}) custom-call(s32[3]{0:T(128)} %pad_add_fusion.core_ref.place_ref, bf16[1024,768]{1,0:T(8,128)(2,1)} %get-tuple-element.122.n_ref, ...), custom_call_target="tpu_custom_call" | custom-call | bytes 1 | tf_op jit(solution)/shard_map/weight_back_kernel/pallas_call | solution.py:713
  186.3 1.4 collective-permute-start.20
  187.7 1.0 collective-permute-start.19
  188.6 6.4 %enter_back_kernel.1 = (f32[512,768]{1,0:T(8,128)}, bf16[512,768]{1,0:T(8,128)(2,1)}) custom-call(s32[3]{0:T(128)} %pad_add_fusion.core_ref.place_ref, bf16[1024,384]{1,0:T(8,128)(2,1)} %get-tuple-element.163.q_ref, bf16[1024,384]{1,0:T(8,128)(2,1)} %get-tuple-element.164.k_ref, bf16[1024,384]{1,0:T(8,128)(2,1)} %get-tuple-element.165.v_ref, ...), custom_call_target="tpu_custom_call" | custom-call | bytes 1 | tf_op jit(solution)/shard_map/enter_back_kernel/pallas_call | solution.py:713
  195.1 2.2 collective-permute-done.24
  197.3 1.2 bitcast_add_fusion.1
  198.5 1.2 bitcast_add_fusion.2
  199.8 1.0 copy-done.42
  201.5 1.1 convert_add_fusion.3
  205.2 1.2 convert_add_fusion.2
  206.4 1.0 convert_add_fusion.4
  208.3 1.5 collective-permute-start.26
  210.6 4.2 %leave_kernel.1 = (f32[512,768]{1,0:T(8,128)}, f32[2,768]{1,0:T(2,128)}) custom-call(bf16[512,768]{1,0:T(8,128)(2,1)} %bitcast.256, f32[512,768]{1,0:T(8,128)} %get-tuple-element.176.gn_ref, bf16[512,768]{1,0:T(8,128)(2,1)} %copy-done.11, f32[512,768]{1,0:T(8,128)} %get-tuple-element.178.gr_ref, f32[8,768]{1,0:T(8,128)} %convert_element_type.149.vec_ref), custom_call_target="tpu_custom_call" | custom-call | bytes 1 | tf_op jit(solution)/shard_map/leave_kernel/pallas_call | solution.py:735
  214.9 1.2 fusion.5
  217.0 2.2 collective-permute-done.32
  219.1 1.2 bitcast_add_fusion
  220.4 2.2 collective-permute-start.35
  222.6 1.2 collective-permute-start.34
  223.8 1.0 bitcast_add_fusion.5
  224.9 1.0 bitcast_add_fusion.6
  226.7 1.7 collective-permute-start.28
  229.3 13.2 %collective-permute-done.29 = f32[10,768]{1,0:T(8,128)S(1)} collective-permute-done((f32[10,768]{1,0:T(8,128)S(1)}, f32[10,768]{1,0:T(8,128)S(1)}, u32[]{:S(2)}, u32[]{:S(2)}) %collective-permute-start.29) | collective-permute-done | bytes 30752 | tf_op jit(solution)/shard_map/ppermute | solution.py:383
  242.5 1.6 collective-permute-start.30
  244.1 2.5 collective-permute-done.30
  246.7 1.5 collective-permute-start.31
  248.2 2.7 collective-permute-done.31
  250.8 1.3 fusion
  252.2 1.1 fusion.6
  253.2 1.0 bitcast_add_fusion.4
  254.3 1.0 bitcast_add_fusion.3
  256.7 2.5 collective-permute-start.36
  260.1 1.2 pad_maximum_fusion.2
  262.0 1.2 reshape.234
  263.2 4.6 %collective-permute-done.36 = bf16[192,384]{1,0:T(8,128)(2,1)S(1)} collective-permute-done((bf16[192,384]{1,0:T(8,128)(2,1)S(1)}, bf16[192,384]{1,0:T(8,128)(2,1)S(1)}, u32[]{:S(2)}, u32[]{:S(2)}) %collective-permute-start.36) | collective-permute-done | bytes 147488 | tf_op jit(solution)/shard_map/ppermute | solution.py:387
  (253 shorter events, 38.3 us)
Async XLA Ops:
  7.2 107.6 %all-gather.3.cloned.1.call-start = ((), (), s32[]{:S(2)}) async-start(), calls=%async_computation | async-start | bytes 5013504 | tf_op jit(solution)/shard_map/all_gather | solution.py:908
  9.7 2.1 copy-start.24
  9.8 1.4 collective-permute-start.10
  11.4 1.4 copy-start.27
  11.7 1.9 copy-start.16
  11.7 1.9 copy-start.17
  13.2 3.4 %collective-permute-start = (bf16[80,384]{1,0:T(8,128)(2,1)S(1)}, bf16[80,384]{1,0:T(8,128)(2,1)S(1)}, u32[]{:S(2)}, u32[]{:S(2)}) collective-permute-start(bf16[80,384]{1,0:T(8,128)(2,1)S(1)} %fusion.24), channel_id=1, source_target_pairs={{0,1},{1,0},{2,3},{3,2},{4,5},{5,4},{6,7},{7,6},{8,9},{9,8},{10,11... | collective-permute-start | bytes 184328 | tf_op jit(solution)/shard_map/ppermute | solution.py:375
  13.8 2.8 %copy-start.28 = (bf16[24,768]{1,0:T(8,128)(2,1)S(1)}, bf16[24,768]{1,0:T(8,128)(2,1)}, u32[]{:S(2)}) copy-start(bf16[24,768]{1,0:T(8,128)(2,1)} %param.24) | copy-start | bytes 110596
  13.9 26.7 %collective-permute-start.4 = (bf16[2,256,768]{2,1,0:T(8,128)(2,1)S(1)}, bf16[2,256,768]{2,1,0:T(8,128)(2,1)S(1)}, u32[]{:S(2)}, u32[]{:S(2)}) collective-permute-start(bf16[2,256,768]{2,1,0:T(8,128)(2,1)S(1)} %pad_maximum_fusion.6), channel_id=1, source_target_pairs={{0,2},{2,0},{1,3},{3,1},{4,6},{6,4},{5,7},{7,5},{8,10},{10,8},{9,1... | collective-permute-start | bytes 2359304 | tf_op jit(solution)/shard_map/ppermute | solution.py:383
  16.7 8.9 %collective-permute-start.3 = (bf16[208,384]{1,0:T(8,128)(2,1)S(1)}, bf16[208,384]{1,0:T(8,128)(2,1)S(1)}, u32[]{:S(2)}, u32[]{:S(2)}) collective-permute-start(bf16[208,384]{1,0:T(8,128)(2,1)S(1)} %pad_maximum_fusion.16), channel_id=1, source_target_pairs={{0,24},{8,16},{16,8},{24,0},{1,25},{9,17},{17,9},{25,1},{2,26},{10... | collective-permute-start | bytes 479240 | tf_op jit(solution)/shard_map/ppermute | solution.py:387
  20.4 20.1 %collective-permute-start.2 = (bf16[208,384]{1,0:T(8,128)(2,1)S(1)}, bf16[208,384]{1,0:T(8,128)(2,1)S(1)}, u32[]{:S(2)}, u32[]{:S(2)}) collective-permute-start(bf16[208,384]{1,0:T(8,128)(2,1)S(1)} %pad_maximum_fusion.16), channel_id=1, source_target_pairs={{0,16},{8,24},{16,0},{24,8},{1,17},{9,25},{17,1},{25,9},{2,18},{10... | collective-permute-start | bytes 479240 | tf_op jit(solution)/shard_map/ppermute | solution.py:387
  20.4 20.1 %collective-permute-start.1 = (bf16[208,384]{1,0:T(8,128)(2,1)S(1)}, bf16[208,384]{1,0:T(8,128)(2,1)S(1)}, u32[]{:S(2)}, u32[]{:S(2)}) collective-permute-start(bf16[208,384]{1,0:T(8,128)(2,1)S(1)} %pad_maximum_fusion.16), channel_id=1, source_target_pairs={{0,8},{8,0},{16,24},{24,16},{1,9},{9,1},{17,25},{25,17},{2,10},{10... | collective-permute-start | bytes 479240 | tf_op jit(solution)/shard_map/ppermute | solution.py:387
  40.7 14.9 %collective-permute-start.6 = (bf16[2,208,384]{2,1,0:T(8,128)(2,1)S(1)}, bf16[2,208,384]{2,1,0:T(8,128)(2,1)S(1)}, u32[]{:S(2)}, u32[]{:S(2)}) collective-permute-start(bf16[2,208,384]{2,1,0:T(8,128)(2,1)S(1)} %get-tuple-element.233), channel_id=1, source_target_pairs={{0,4},{4,0},{1,5},{5,1},{2,6},{6,2},{3,7},{7,3},{8,12},{12,8},{9,1... | collective-permute-start | bytes 958472 | tf_op jit(solution)/shard_map/ppermute | solution.py:379
  42.3 13.1 %collective-permute-start.8 = (bf16[2,208,384]{2,1,0:T(8,128)(2,1)S(1)}, bf16[2,208,384]{2,1,0:T(8,128)(2,1)S(1)}, u32[]{:S(2)}, u32[]{:S(2)}) collective-permute-start(bf16[2,208,384]{2,1,0:T(8,128)(2,1)S(1)} %get-tuple-element.234), channel_id=1, source_target_pairs={{0,2},{2,0},{1,3},{3,1},{4,6},{6,4},{5,7},{7,5},{8,10},{10,8},{9,1... | collective-permute-start | bytes 958472 | tf_op jit(solution)/shard_map/ppermute | solution.py:383
  55.5 15.2 %collective-permute-start.9 = (bf16[2,2,208,384]{3,2,0,1:T(8,128)(2,1)S(1)}, bf16[2,2,208,384]{3,2,0,1:T(8,128)(2,1)S(1)}, u32[]{:S(2)}, u32[]{:S(2)}) collective-permute-start(bf16[2,2,208,384]{3,2,0,1:T(8,128)(2,1)S(1)} %pad_maximum_fusion.10), channel_id=1, source_target_pairs={{0,4},{4,0},{1,5},{5,1},{2,6},{6,2},{3,7},{7,3},{8,12},{12,8},{9,1... | collective-permute-start | bytes 1916936 | tf_op jit(solution)/shard_map/ppermute | solution.py:379
  55.7 15.3 %collective-permute-start.7 = (bf16[2,2,208,384]{3,2,1,0:T(8,128)(2,1)S(1)}, bf16[2,2,208,384]{3,2,1,0:T(8,128)(2,1)S(1)}, u32[]{:S(2)}, u32[]{:S(2)}) collective-permute-start(bf16[2,2,208,384]{3,2,1,0:T(8,128)(2,1)S(1)} %pad_maximum_fusion.9), channel_id=1, source_target_pairs={{0,2},{2,0},{1,3},{3,1},{4,6},{6,4},{5,7},{7,5},{8,10},{10,8},{9,1... | collective-permute-start | bytes 1916936 | tf_op jit(solution)/shard_map/ppermute | solution.py:383
  58.2 12.6 %copy-start.1 = (bf16[1,2,256,768]{3,2,0,1:T(8,128)(2,1)}, bf16[1,2,256,768]{3,2,0,1:T(8,128)(2,1)S(1)}, u32[]{:S(2)}) copy-start(bf16[1,2,256,768]{3,2,0,1:T(8,128)(2,1)S(1)} %get-tuple-element.214) | copy-start | bytes 2359300
  58.2 16.6 %collective-permute-start.5 = (bf16[512,768]{1,0:T(8,128)(2,1)S(1)}, bf16[512,768]{1,0:T(8,128)(2,1)S(1)}, u32[]{:S(2)}, u32[]{:S(2)}) collective-permute-start(bf16[512,768]{1,0:T(8,128)(2,1)S(1)} %bitcast.253), channel_id=1, source_target_pairs={{0,1},{1,0},{2,3},{3,2},{4,5},{5,4},{6,7},{7,6},{8,9},{9,8},{10,11... | collective-permute-start | bytes 2359304 | tf_op jit(solution)/shard_map/ppermute | solution.py:375
  71.5 1.5 copy-start
  73.1 30.1 %collective-permute-start.11 = (bf16[8,24,768]{2,1,0:T(8,128)(2,1)S(1)}, bf16[8,24,768]{2,1,0:T(8,128)(2,1)S(1)}, u32[]{:S(2)}, u32[]{:S(2)}) collective-permute-start(bf16[8,24,768]{2,1,0:T(8,128)(2,1)S(1)} %dynamic-slice_bitcast_fusion.3), channel_id=1, source_target_pairs={{0,1},{1,0},{2,3},{3,2},{4,5},{5,4},{6,7},{7,6},{8,9},{9,8},{10,11... | collective-permute-start | bytes 884744 | tf_op jit(solution)/shard_map/ppermute | solution.py:375
  73.3 8.9 %copy-start.20 = (f32[32,8,24]{2,1,0:T(8,128)}, f32[32,8,24]{2,1,0:T(8,128)S(1)}, u32[]{:S(2)}) copy-start(f32[32,8,24]{2,1,0:T(8,128)S(1)} %reshape.240) | copy-start | bytes 73732
  103.3 5.0 %copy-start.4 = (bf16[1,2,256,768]{3,2,0,1:T(8,128)(2,1)S(1)}, bf16[1,2,256,768]{3,2,0,1:T(8,128)(2,1)}, u32[]{:S(2)}) copy-start(bf16[1,2,256,768]{3,2,0,1:T(8,128)(2,1)} %get-tuple-element.213) | copy-start | bytes 2359300
  107.7 3.2 %collective-permute-start.12 = (bf16[512,768]{1,0:T(8,128)(2,1)}, bf16[512,768]{1,0:T(8,128)(2,1)S(1)}, u32[]{:S(2)}, u32[]{:S(2)}) collective-permute-start(bf16[512,768]{1,0:T(8,128)(2,1)} %get-tuple-element.128), channel_id=1, source_target_pairs={{0,1},{1,0},{2,3},{3,2},{4,5},{5,4},{6,7},{7,6},{8,9},{9,8},{10,11... | collective-permute-start | bytes 2359304 | tf_op jit(solution)/shard_map/ppermute | solution.py:375
  108.3 7.7 %collective-permute-start.14 = (bf16[512,768]{1,0:T(8,128)(2,1)S(1)}, bf16[512,768]{1,0:T(8,128)(2,1)S(1)}, u32[]{:S(2)}, u32[]{:S(2)}) collective-permute-start(bf16[512,768]{1,0:T(8,128)(2,1)S(1)} %bitcast.263), channel_id=1, source_target_pairs={{0,1},{1,0},{2,3},{3,2},{4,5},{5,4},{6,7},{7,6},{8,9},{9,8},{10,11... | collective-permute-start | bytes 2359304 | tf_op jit(solution)/shard_map/ppermute | solution.py:375
  114.8 2.5 collective-permute-start.13
  140.6 2.9 %collective-permute-start.17 = (bf16[512,768]{1,0:T(8,128)(2,1)}, bf16[512,768]{1,0:T(8,128)(2,1)S(1)}, u32[]{:S(2)}, u32[]{:S(2)}) collective-permute-start(bf16[512,768]{1,0:T(8,128)(2,1)} %get-tuple-element.137), channel_id=1, source_target_pairs={{0,1},{1,0},{2,3},{3,2},{4,5},{5,4},{6,7},{7,6},{8,9},{9,8},{10,11... | collective-permute-start | bytes 2359304 | tf_op jit(solution)/shard_map/ppermute | solution.py:375
  141.0 29.4 %collective-permute-start.15 = (bf16[8,48,1536]{2,1,0:T(8,128)(2,1)}, bf16[8,48,1536]{2,1,0:T(8,128)(2,1)S(1)}, u32[]{:S(2)}, u32[]{:S(2)}) collective-permute-start(bf16[8,48,1536]{2,1,0:T(8,128)(2,1)} %get-tuple-element.133), channel_id=1, source_target_pairs={{0,2},{2,0},{1,3},{3,1},{4,6},{6,4},{5,7},{7,5},{8,10},{10,8},{9,1... | collective-permute-start | bytes 3538952 | tf_op jit(solution)/shard_map/ppermute | solution.py:383
  142.1 28.4 %collective-permute-start.16 = (bf16[4,2,96,768]{3,2,1,0:T(8,128)(2,1)}, bf16[4,2,96,768]{3,2,1,0:T(8,128)(2,1)S(1)}, u32[]{:S(2)}, u32[]{:S(2)}) collective-permute-start(bf16[4,2,96,768]{3,2,1,0:T(8,128)(2,1)} %get-tuple-element.134), channel_id=1, source_target_pairs={{0,4},{4,0},{1,5},{5,1},{2,6},{6,2},{3,7},{7,3},{8,12},{12,8},{9,1... | collective-permute-start | bytes 3538952 | tf_op jit(solution)/shard_map/ppermute | solution.py:379
  148.6 2.5 collective-permute-start.18
  157.4 19.4 %collective-permute-start.23 = (bf16[8,24,768]{2,1,0:T(8,128)(2,1)S(1)}, bf16[8,24,768]{2,1,0:T(8,128)(2,1)S(1)}, u32[]{:S(2)}, u32[]{:S(2)}) collective-permute-start(bf16[8,24,768]{2,1,0:T(8,128)(2,1)S(1)} %dynamic-slice_bitcast_fusion.2), channel_id=1, source_target_pairs={{0,1},{1,0},{2,3},{3,2},{4,5},{5,4},{6,7},{7,6},{8,9},{9,8},{10,11... | collective-permute-start | bytes 884744 | tf_op jit(solution)/shard_map/ppermute | solution.py:375
  157.6 13.9 %copy-start.8 = (bf16[8,48,1536]{2,1,0:T(8,128)(2,1)S(1)}, bf16[8,48,1536]{2,1,0:T(8,128)(2,1)}, u32[]{:S(2)}) copy-start(bf16[8,48,1536]{2,1,0:T(8,128)(2,1)} %get-tuple-element.132) | copy-start | bytes 3538948
  171.6 1.6 copy-start.10
  173.4 3.5 %copy-start.2 = (f32[4,2,96,768]{3,2,1,0:T(8,128)}, f32[4,2,96,768]{3,2,1,0:T(8,128)S(1)}, u32[]{:S(2)}) copy-start(f32[4,2,96,768]{3,2,1,0:T(8,128)S(1)} %convert_add_fusion) | copy-start | bytes 7077892
  173.4 3.4 %copy-start.22 = (bf16[384,768]{1,0:T(8,128)(2,1)S(1)}, bf16[384,768]{1,0:T(8,128)(2,1)}, u32[]{:S(2)}) copy-start(bf16[384,768]{1,0:T(8,128)(2,1)} %get-tuple-element.162) | copy-start | bytes 1769476
  174.5 22.8 %collective-permute-start.21 = (bf16[4,48,1536]{2,1,0:T(8,128)(2,1)}, bf16[4,48,1536]{2,1,0:T(8,128)(2,1)}, u32[]{:S(2)}, u32[]{:S(2)}) collective-permute-start(bf16[4,48,1536]{2,1,0:T(8,128)(2,1)} %fusion.3), channel_id=1, source_target_pairs={{0,4},{4,0},{1,5},{5,1},{2,6},{6,2},{3,7},{7,3},{8,12},{12,8},{9,1... | collective-permute-start | bytes 1769480 | tf_op jit(solution)/shard_map/ppermute | solution.py:379
  175.8 21.5 %collective-permute-start.22 = (bf16[4,96,768]{2,1,0:T(8,128)(2,1)S(1)}, bf16[4,96,768]{2,1,0:T(8,128)(2,1)}, u32[]{:S(2)}, u32[]{:S(2)}) collective-permute-start(bf16[4,96,768]{2,1,0:T(8,128)(2,1)S(1)} %fusion.2), channel_id=1, source_target_pairs={{0,2},{2,0},{1,3},{3,1},{4,6},{6,4},{5,7},{7,5},{8,10},{10,8},{9,1... | collective-permute-start | bytes 1769480 | tf_op jit(solution)/shard_map/ppermute | solution.py:383
  177.7 19.6 %collective-permute-start.24 = (bf16[4,2,24,768]{3,2,1,0:T(8,128)(2,1)}, bf16[4,2,24,768]{3,2,1,0:T(8,128)(2,1)}, u32[]{:S(2)}, u32[]{:S(2)}) collective-permute-start(bf16[4,2,24,768]{3,2,1,0:T(8,128)(2,1)} %dynamic-slice_bitcast_fusion.1), channel_id=1, source_target_pairs={{0,4},{4,0},{1,5},{5,1},{2,6},{6,2},{3,7},{7,3},{8,12},{12,8},{9,1... | collective-permute-start | bytes 884744 | tf_op jit(solution)/shard_map/ppermute | solution.py:379
  186.3 11.0 %copy-start.3 = (f32[4,2,96,768]{3,2,1,0:T(8,128)S(1)}, f32[4,2,96,768]{3,2,1,0:T(8,128)}, u32[]{:S(2)}) copy-start(f32[4,2,96,768]{3,2,1,0:T(8,128)} %copy-done.2) | copy-start | bytes 7077892
  186.3 18.4 %collective-permute-start.20 = (bf16[4,2,48,384]{3,2,1,0:T(8,128)(2,1)}, bf16[4,2,48,384]{3,2,1,0:T(8,128)(2,1)}, u32[]{:S(2)}, u32[]{:S(2)}) collective-permute-start(bf16[4,2,48,384]{3,2,1,0:T(8,128)(2,1)} %get-tuple-element.159), channel_id=1, source_target_pairs={{0,4},{4,0},{1,5},{5,1},{2,6},{6,2},{3,7},{7,3},{8,12},{12,8},{9,1... | collective-permute-start | bytes 884744 | tf_op jit(solution)/shard_map/ppermute | solution.py:379
  187.7 17.0 %collective-permute-start.19 = (bf16[8,96,384]{2,1,0:T(8,128)(2,1)}, bf16[8,96,384]{2,1,0:T(8,128)(2,1)}, u32[]{:S(2)}, u32[]{:S(2)}) collective-permute-start(bf16[8,96,384]{2,1,0:T(8,128)(2,1)} %get-tuple-element.158), channel_id=1, source_target_pairs={{0,2},{2,0},{1,3},{3,1},{4,6},{6,4},{5,7},{7,5},{8,10},{10,8},{9,1... | collective-permute-start | bytes 1769480 | tf_op jit(solution)/shard_map/ppermute | solution.py:383
  197.3 6.8 %collective-permute-start.33 = (bf16[512,768]{1,0:T(8,128)(2,1)}, bf16[512,768]{1,0:T(8,128)(2,1)S(1)}, u32[]{:S(2)}, u32[]{:S(2)}) collective-permute-start(bf16[512,768]{1,0:T(8,128)(2,1)} %get-tuple-element.191), channel_id=1, source_target_pairs={{0,1},{1,0},{2,3},{3,2},{4,5},{5,4},{6,7},{7,6},{8,9},{9,8},{10,11... | collective-permute-start | bytes 2359304 | tf_op jit(solution)/shard_map/ppermute | solution.py:375
  200.8 3.9 %collective-permute-start.25 = (bf16[512,768]{1,0:T(8,128)(2,1)S(1)}, bf16[512,768]{1,0:T(8,128)(2,1)S(1)}, u32[]{:S(2)}, u32[]{:S(2)}) collective-permute-start(bf16[512,768]{1,0:T(8,128)(2,1)S(1)} %copy-done.42), channel_id=1, source_target_pairs={{0,1},{1,0},{2,3},{3,2},{4,5},{5,4},{6,7},{7,6},{8,9},{9,8},{10,11... | collective-permute-start | bytes 2359304 | tf_op jit(solution)/shard_map/ppermute | solution.py:375
  201.5 2.5 copy-start.6
  202.7 1.7 copy-start.5
  202.7 1.7 copy-start.29
  203.6 15.6 %collective-permute-start.32 = (bf16[2,192,768]{2,1,0:T(8,128)(2,1)}, bf16[2,192,768]{2,1,0:T(8,128)(2,1)}, u32[]{:S(2)}, u32[]{:S(2)}) collective-permute-start(bf16[2,192,768]{2,1,0:T(8,128)(2,1)} %fusion.4), channel_id=1, source_target_pairs={{0,8},{8,0},{16,24},{24,16},{1,9},{9,1},{17,25},{25,17},{2,10},{10... | collective-permute-start | bytes 1769480 | tf_op jit(solution)/shard_map/ppermute | solution.py:387
  204.7 1.7 copy-start.23
  204.7 1.6 copy-start.11
  208.3 15.5 %collective-permute-start.26 = (bf16[4,96,384]{2,1,0:T(8,128)(2,1)}, bf16[4,96,384]{2,1,0:T(8,128)(2,1)}, u32[]{:S(2)}, u32[]{:S(2)}) collective-permute-start(bf16[4,96,384]{2,1,0:T(8,128)(2,1)} %fusion.12), channel_id=1, source_target_pairs={{0,4},{4,0},{1,5},{5,1},{2,6},{6,2},{3,7},{7,3},{8,12},{12,8},{9,1... | collective-permute-start | bytes 884744 | tf_op jit(solution)/shard_map/ppermute | solution.py:379
  209.8 14.0 %collective-permute-start.27 = (bf16[4,96,384]{2,1,0:T(8,128)(2,1)S(1)}, bf16[4,96,384]{2,1,0:T(8,128)(2,1)}, u32[]{:S(2)}, u32[]{:S(2)}) collective-permute-start(bf16[4,96,384]{2,1,0:T(8,128)(2,1)S(1)} %fusion.10), channel_id=1, source_target_pairs={{0,2},{2,0},{1,3},{3,1},{4,6},{6,4},{5,7},{7,5},{8,10},{10,8},{9,1... | collective-permute-start | bytes 884744 | tf_op jit(solution)/shard_map/ppermute | solution.py:383
  220.3 4.5 %copy-start.30 = (f32[4,768]{1,0:T(4,128)S(1)}, f32[4,768]{1,0:T(4,128)}, u32[]{:S(2)}) copy-start(f32[4,768]{1,0:T(4,128)} %get-tuple-element.183) | copy-start | bytes 36868
  220.4 4.5 %copy-start.31 = (f32[2,768]{1,0:T(2,128)S(1)}, f32[2,768]{1,0:T(2,128)}, u32[]{:S(2)}) copy-start(f32[2,768]{1,0:T(2,128)} %get-tuple-element.182) | copy-start | bytes 18436
  220.4 4.5 %copy-start.32 = (f32[2,768]{1,0:T(2,128)S(1)}, f32[2,768]{1,0:T(2,128)}, u32[]{:S(2)}) copy-start(f32[2,768]{1,0:T(2,128)} %get-tuple-element.184) | copy-start | bytes 18436
  220.4 27.7 %collective-permute-start.35 = (bf16[192,768]{1,0:T(8,128)(2,1)S(1)}, bf16[192,768]{1,0:T(8,128)(2,1)}, u32[]{:S(2)}, u32[]{:S(2)}) collective-permute-start(bf16[192,768]{1,0:T(8,128)(2,1)S(1)} %fusion.11), channel_id=1, source_target_pairs={{0,16},{8,24},{16,0},{24,8},{1,17},{9,25},{17,1},{25,9},{2,18},{10... | collective-permute-start | bytes 884744 | tf_op jit(solution)/shard_map/ppermute | solution.py:387
  222.6 28.2 %collective-permute-start.34 = (bf16[512,768]{1,0:T(8,128)(2,1)}, bf16[512,768]{1,0:T(8,128)(2,1)}, u32[]{:S(2)}, u32[]{:S(2)}) collective-permute-start(bf16[512,768]{1,0:T(8,128)(2,1)} %pad_maximum_fusion.7), channel_id=1, source_target_pairs={{0,2},{2,0},{1,3},{3,1},{4,6},{6,4},{5,7},{7,5},{8,10},{10,8},{9,1... | collective-permute-start | bytes 2359304 | tf_op jit(solution)/shard_map/ppermute | solution.py:383
  226.7 24.1 %collective-permute-start.28 = (bf16[2,192,384]{2,1,0:T(8,128)(2,1)}, bf16[2,192,384]{2,1,0:T(8,128)(2,1)}, u32[]{:S(2)}, u32[]{:S(2)}) collective-permute-start(bf16[2,192,384]{2,1,0:T(8,128)(2,1)} %fusion.13), channel_id=1, source_target_pairs={{0,8},{8,0},{16,24},{24,16},{1,9},{9,1},{17,25},{25,17},{2,10},{10... | collective-permute-start | bytes 884744 | tf_op jit(solution)/shard_map/ppermute | solution.py:387
  228.5 14.0 %collective-permute-start.29 = (f32[10,768]{1,0:T(8,128)S(1)}, f32[10,768]{1,0:T(8,128)S(1)}, u32[]{:S(2)}, u32[]{:S(2)}) collective-permute-start(f32[10,768]{1,0:T(8,128)S(1)} %pad_maximum_fusion.22), channel_id=1, source_target_pairs={{0,2},{2,0},{1,3},{3,1},{4,6},{6,4},{5,7},{7,5},{8,10},{10,8},{9,1... | collective-permute-start | bytes 92168 | tf_op jit(solution)/shard_map/ppermute | solution.py:383
  242.5 4.2 %collective-permute-start.30 = (f32[10,768]{1,0:T(8,128)S(1)}, f32[10,768]{1,0:T(8,128)S(1)}, u32[]{:S(2)}, u32[]{:S(2)}) collective-permute-start(f32[10,768]{1,0:T(8,128)S(1)} %add.187), channel_id=1, source_target_pairs={{0,4},{4,0},{1,5},{5,1},{2,6},{6,2},{3,7},{7,3},{8,12},{12,8},{9,1... | collective-permute-start | bytes 92168 | tf_op jit(solution)/shard_map/ppermute | solution.py:379
  246.7 4.2 %collective-permute-start.31 = (f32[10,768]{1,0:T(8,128)S(1)}, f32[10,768]{1,0:T(8,128)S(1)}, u32[]{:S(2)}, u32[]{:S(2)}) collective-permute-start(f32[10,768]{1,0:T(8,128)S(1)} %add.188), channel_id=1, source_target_pairs={{0,8},{8,0},{16,24},{24,16},{1,9},{9,1},{17,25},{25,17},{2,10},{10... | collective-permute-start | bytes 92168 | tf_op jit(solution)/shard_map/ppermute | solution.py:387
  256.1 7.2 %collective-permute-start.37 = (f32[10,768]{1,0:T(8,128)S(1)}, f32[10,768]{1,0:T(8,128)S(1)}, u32[]{:S(2)}, u32[]{:S(2)}) collective-permute-start(f32[10,768]{1,0:T(8,128)S(1)} %add.199), channel_id=1, source_target_pairs={{0,16},{8,24},{16,0},{24,8},{1,17},{9,25},{17,1},{25,9},{2,18},{10... | collective-permute-start | bytes 92168 | tf_op jit(solution)/shard_map/ppermute | solution.py:387
  256.6 4.8 %collective-permute-start.38 = (f32[2,24,768]{2,1,0:T(8,128)S(1)}, f32[2,24,768]{2,1,0:T(8,128)S(1)}, u32[]{:S(2)}, u32[]{:S(2)}) collective-permute-start(f32[2,24,768]{2,1,0:T(8,128)S(1)} %dynamic-slice_bitcast_fusion.4), channel_id=1, source_target_pairs={{0,1},{1,0},{2,3},{3,2},{4,5},{5,4},{6,7},{7,6},{8,9},{9,8},{10,11... | collective-permute-start | bytes 442376 | tf_op jit(solution)/shard_map/ppermute | solution.py:375
  256.7 11.2 %collective-permute-start.36 = (bf16[192,384]{1,0:T(8,128)(2,1)S(1)}, bf16[192,384]{1,0:T(8,128)(2,1)S(1)}, u32[]{:S(2)}, u32[]{:S(2)}) collective-permute-start(bf16[192,384]{1,0:T(8,128)(2,1)S(1)} %fusion.18), channel_id=1, source_target_pairs={{0,16},{8,24},{16,0},{24,8},{1,17},{9,25},{17,1},{25,9},{2,18},{10... | collective-permute-start | bytes 442376 | tf_op jit(solution)/shard_map/ppermute | solution.py:387
  268.0 1.9 collective-permute-start.40
  268.1 2.4 collective-permute-start.39
  (21 other events, 24.3 us)
Sparse Core Ops, SparseCore 0:
  12.7 92.1 all-gather.2

commit v2 on v1

--- a/solution.py
+++ b/solution.py
@@ -1037,8 +1037,6 @@
     output = output.astype(BF).reshape(2, block, width)
     grad_tokens = grad_tokens.reshape(2, block, width)
     to_y = jnp.concatenate((pick(output, 1 - y, 0), pick(grad_tokens, 1 - y, 0).astype(BF)))
-    forward_from, to_y = lax.optimization_barrier((forward_from, to_y))
-    from_y = other_y(to_y)
     forward_kept, forward_from = second_z(plus(forward_kept, forward_from))
 
     left_from, right_from, sums1 = lax.optimization_barrier((left_from, right_from, sums1))
@@ -1049,11 +1047,11 @@
     last, small_grads = lax.optimization_barrier((last, small_grads))
     last, last_from = first_z(last)
     small_grads = small_grads + other_y(small_grads)
+    small_grads, to_y = lax.optimization_barrier((small_grads, to_y))
+    from_y = other_y(to_y)
     small_grads = small_grads + other_x(small_grads)
     small_from = other_z(small_grads, 1)
-    last_from, small_from, from_y, forward_from = lax.optimization_barrier(
-        (last_from, small_from, from_y, forward_from)
-    )
+    last_from, small_from, forward_from = lax.optimization_barrier((last_from, small_from, forward_from))
     last, last_from = second_z(plus(last, last_from))
     small_grads = small_grads + small_from
     small_from = other_z(small_grads, 2)

time: 282 us -> 277 us (0.982)
  waiting for transfers between devices: 77.7 us -> 71.8 us
    ppermute x9, waiting for transfers between devices: 25.1 us -> 18.4 us  [other_y(): return lax.ppermute(value, 'y', [(0, 1), (1, 0)])]
    unnamed x94 -> x104, local copies, waits for them, and re-layouts: 11.6 us -> 13 us
  transfers between devices with their start and end apart: 42 -> 42, of which waited for: 14 -> 14; matrix products, arithmetic and copies ran while one was open for 12% -> 13% of each run, Pallas kernels for 26% -> 26%
where the time goes in v2:
time: 277 us; the launch traced here: 274 us
  Pallas kernels  94.2 us (34%)
  waiting for transfers between devices  71.8 us (26%)
  starting transfers between devices  37 us (13%)
  local copies, waits for them, and re-layouts  32 us (12%)
  other arithmetic  23.6 us (9%)
  between operations  15.7 us (6%)
    ppermute x9, waiting for transfers between devices, other_z(): lax.ppermute(value, 'z', [(i, i ^ by) for i in range(lax.axis_size('z'))])  28.9 us
    pallas_call x5, Pallas kernels, whole_call(): pl.pallas_call(kernel, in_specs=in_specs, out_specs=[pl.BlockSpec(memory_...  26.5 us
    pallas_call x1, Pallas kernels, feed_forward(): pl.pallas_call(hidden_kernel, grid=(steps,), in_specs=[pl.BlockSpec(memor...  22.4 us
    pallas_call x1, Pallas kernels, attend(): pl.pallas_call(attend_kernel, grid=(pairs,), in_specs=[block] * 3, out_sp...  21 us
    ppermute x9, waiting for transfers between devices, other_y(): return lax.ppermute(value, 'y', [(0, 1), (1, 0)])  18.4 us
    ppermute x8, waiting for transfers between devices, other_x(): return lax.ppermute(value, 'x', [(0, 1), (1, 0)])  17.3 us
    unnamed x104, local copies, waits for them, and re-layouts  13 us
    pallas_call x1, Pallas kernels, attend_back(): pl.pallas_call(attend_back_kernel, grid=(pairs,), in_specs=[block] * 5 +...  12.8 us
  transfers between devices with their start and end apart: 42, of which 14 were waited for; matrix products, arithmetic and copies ran while one was open for 13% of the time, Pallas kernels for 26%

profile of v2, /device:TPU:0, one launch (start us, length us, event | category | flops | bytes accessed | tf_op | source)
XLA Modules:
  0.0 274.4 jit_solution(7658206389095689494)
XLA Ops:
  7.2 1.1 reshape.217
  8.4 1.3 dynamic-slice_reduce_fusion.1
  13.9 2.7 collective-permute-start.4
  16.7 3.7 %collective-permute-start.3 = (bf16[208,384]{1,0:T(8,128)(2,1)S(1)}, bf16[208,384]{1,0:T(8,128)(2,1)S(1)}, u32[]{:S(2)}, u32[]{:S(2)}) collective-permute-start(bf16[208,384]{1,0:T(8,128)(2,1)S(1)} %pad_maximum_fusion.16), channel_id=1, source_target_pairs={{0,24},{8,16},{16,8},{24,0},{1,25},{9,17},{17,9},{25,1},{2,26},{10... | collective-permute-start | bytes 479240 | tf_op jit(solution)/shard_map/ppermute | solution.py:387
  21.8 3.9 %collective-permute-done.3 = bf16[208,384]{1,0:T(8,128)(2,1)S(1)} collective-permute-done((bf16[208,384]{1,0:T(8,128)(2,1)S(1)}, bf16[208,384]{1,0:T(8,128)(2,1)S(1)}, u32[]{:S(2)}, u32[]{:S(2)}) %collective-permute-start.3) | collective-permute-done | bytes 159776 | tf_op jit(solution)/shard_map/ppermute | solution.py:387
  25.7 14.8 %collective-permute-done.2 = bf16[208,384]{1,0:T(8,128)(2,1)S(1)} collective-permute-done((bf16[208,384]{1,0:T(8,128)(2,1)S(1)}, bf16[208,384]{1,0:T(8,128)(2,1)S(1)}, u32[]{:S(2)}, u32[]{:S(2)}) %collective-permute-start.2) | collective-permute-done | bytes 159776 | tf_op jit(solution)/shard_map/ppermute | solution.py:387
  40.7 1.6 collective-permute-start.6
  43.4 11.9 %collective-permute-done.8 = bf16[2,208,384]{2,1,0:T(8,128)(2,1)S(1)} collective-permute-done((bf16[2,208,384]{2,1,0:T(8,128)(2,1)S(1)}, bf16[2,208,384]{2,1,0:T(8,128)(2,1)S(1)}, u32[]{:S(2)}, u32[]{:S(2)}) %collective-permute-start.8) | collective-permute-done | bytes 319520 | tf_op jit(solution)/shard_map/ppermute | solution.py:383
  55.7 1.5 collective-permute-start.7
  57.2 1.0 fusion.27
  58.2 12.5 %collective-permute-done.9 = bf16[2,2,208,384]{3,2,0,1:T(8,128)(2,1)S(1)} collective-permute-done((bf16[2,2,208,384]{3,2,0,1:T(8,128)(2,1)S(1)}, bf16[2,2,208,384]{3,2,0,1:T(8,128)(2,1)S(1)}, u32[]{:S(2)}, u32[]{:S(2)}) %collective-permute-start.9) | collective-permute-done | bytes 639008 | tf_op jit(solution)/shard_map/ppermute | solution.py:379
  71.6 1.3 copy-done
  75.7 6.5 %enter_kernel.1 = (bf16[1024,768]{1,0:T(8,128)(2,1)}, bf16[1024,384]{1,0:T(8,128)(2,1)}, bf16[1024,384]{1,0:T(8,128)(2,1)}, bf16[1024,384]{1,0:T(8,128)(2,1)}) custom-call(s32[3]{0:T(128)} %pad_add_fusion.core_ref.place_ref, bf16[512,768]{1,0:T(8,128)(2,1)} %bitcast.254, bf16[512,768]{1,0:T(8,128)(2,1)} %copy-done.13, ...), custom_call_target="tpu_custom_call" | custom-call | bytes 1 | tf_op jit(solution)/shard_map/enter_kernel/pallas_call | solution.py:713
  82.1 21.0 %attend.1 = (bf16[1024,384]{1,0:T(8,128)(2,1)}, f32[3,2,1024]{2,1,0:T(2,128)}) custom-call(bf16[1024,384]{1,0:T(8,128)(2,1)} %get-tuple-element.122.q_ref, bf16[1024,384]{1,0:T(8,128)(2,1)} %get-tuple-element.123.k_ref, bf16[1024,384]{1,0:T(8,128)(2,1)} %get-tuple-element.124.v_ref), custom_call_target="tpu_custom_call" | custom-call | bytes 1 | tf_op jit(solution)/shard_map/attend/pallas_call | solution.py:526
  104.1 3.5 %out_kernel.1 = (f32[512,768]{1,0:T(8,128)}, bf16[512,768]{1,0:T(8,128)(2,1)}) custom-call(s32[3]{0:T(128)} %pad_add_fusion.core_ref.place_ref, bf16[1024,384]{1,0:T(8,128)(2,1)} %get-tuple-element.125.mixed_ref, bf16[384,768]{1,0:T(8,128)(2,1)} %bitcast.264), custom_call_target="tpu_custom_call" | custom-call | bytes 1 | tf_op jit(solution)/shard_map/out_kernel/pallas_call | solution.py:713
  108.3 2.5 collective-permute-done.12.received_ref
  111.7 3.0 %middle_kernel.1 = (f32[512,768]{1,0:T(8,128)}, bf16[512,768]{1,0:T(8,128)(2,1)}) custom-call(bf16[512,768]{1,0:T(8,128)(2,1)} %bitcast.255, f32[512,768]{1,0:T(8,128)} %get-tuple-element.126.part_ref, bf16[512,768]{1,0:T(8,128)(2,1)} %copy-done.20, f32[8,768]{1,0:T(8,128)} %convert_element_type.149.vec_ref), custom_call_target="tpu_custom_call" | custom-call | bytes 1 | tf_op jit(solution)/shard_map/middle_kernel/pallas_call | solution.py:735
  115.9 1.3 collective-permute-done.13.n_other
  118.1 22.4 %feed_forward.1 = (f32[512,768]{1,0:T(8,128)}, bf16[512,768]{1,0:T(8,128)(2,1)}, f32[512,768]{1,0:T(8,128)}, bf16[512,768]{1,0:T(8,128)(2,1)}, bf16[8,48,1536]{2...) custom-call(s32[3]{0:T(128)} %pad_add_fusion.core_ref.place_ref, ...), custom_call_target="tpu_custom_call" | custom-call | bytes 1 | tf_op jit(solution)/shard_map/feed_forward/pallas_call | solution.py:812
  141.0 1.1 collective-permute-start.15
  142.0 1.5 collective-permute-start.16
  144.4 4.3 %middle_back_kernel.1 = (f32[512,768]{1,0:T(8,128)}, bf16[512,768]{1,0:T(8,128)(2,1)}, f32[4,768]{1,0:T(4,128)}) custom-call(f32[512,768]{1,0:T(8,128)} %get-tuple-element.134.residual_ref, f32[512,768]{1,0:T(8,128)} %get-tuple-element.135.gn_ref, bf16[512,768]{1,0:T(8,128)(2,1)} %copy-done.16, bf16[512,768]{1,0:T(8,128)(2,1)} %bitcast.262, ...), custom_call_target="tpu_custom_call" | custom-call | bytes 1 | tf_op jit(solution)/shard_map/middle_back_kernel/pallas_call | solution.py:735
  148.7 2.5 collective-permute-done.18.other_ref
  152.1 4.4 %mixed_back_kernel.1 = (bf16[1024,384]{1,0:T(8,128)(2,1)}, bf16[384,768]{1,0:T(8,128)(2,1)}) custom-call(s32[3]{0:T(128)} %pad_add_fusion.core_ref.place_ref, bf16[1024,384]{1,0:T(8,128)(2,1)} %get-tuple-element.125.mixed_ref, bf16[512,768]{1,0:T(8,128)(2,1)} %get-tuple-element.137.mine_ref, bf16[512,768]{1,0:T(8,128)(2,1)} %copy-done.19, ...), custom_call_target="tpu_custom_call" | custom-call | bytes 1 | tf_op jit(solution)/shard_map/mixed_back_kernel/pallas_call | solution.py:713
  156.5 1.0 dynamic-slice_bitcast_fusion.2
  157.7 12.8 %attend_back.1 = (bf16[1024,384]{1,0:T(8,128)(2,1)}, bf16[1024,384]{1,0:T(8,128)(2,1)}, bf16[1024,384]{1,0:T(8,128)(2,1)}) custom-call(bf16[1024,384]{1,0:T(8,128)(2,1)} %get-tuple-element.122.q_ref, bf16[1024,384]{1,0:T(8,128)(2,1)} %get-tuple-element.123.k_ref, bf16[1024,384]{1,0:T(8,128)(2,1)} %get-tuple-element.124.v_ref, ...), custom_call_target="tpu_custom_call" | custom-call | bytes 1 | tf_op jit(solution)/shard_map/attend_back/pallas_call | solution.py:546
  170.6 1.1 copy-done.9
  172.0 0.9 copy-done.7
  174.5 1.2 collective-permute-start.21
  175.8 1.1 collective-permute-start.22
  178.4 1.0 slice_reduce_fusion
  180.7 5.6 %weight_back_kernel.1 = (bf16[8,96,384]{2,1,0:T(8,128)(2,1)}, bf16[8,96,384]{2,1,0:T(8,128)(2,1)}, bf16[4,2,48,384]{3,2,1,0:T(8,128)(2,1)}, bf16[4,2,48,384]{3,2,1,0:T(8,128)(2,1)}, f32[2,768]{1,0:T(2,128)}) custom-call(s32[3]{0:T(128)} %pad_add_fusion.core_ref.place_ref, bf16[1024,768]{1,0:T(8,128)(2,1)} %get-tuple-element.121.n_ref, ...), custom_call_target="tpu_custom_call" | custom-call | bytes 1 | tf_op jit(solution)/shard_map/weight_back_kernel/pallas_call | solution.py:713
  186.3 1.4 collective-permute-start.20
  188.7 6.4 %enter_back_kernel.1 = (f32[512,768]{1,0:T(8,128)}, bf16[512,768]{1,0:T(8,128)(2,1)}) custom-call(s32[3]{0:T(128)} %pad_add_fusion.core_ref.place_ref, bf16[1024,384]{1,0:T(8,128)(2,1)} %get-tuple-element.162.q_ref, bf16[1024,384]{1,0:T(8,128)(2,1)} %get-tuple-element.163.k_ref, bf16[1024,384]{1,0:T(8,128)(2,1)} %get-tuple-element.164.v_ref, ...), custom_call_target="tpu_custom_call" | custom-call | bytes 1 | tf_op jit(solution)/shard_map/enter_back_kernel/pallas_call | solution.py:713
  195.1 2.3 collective-permute-done.24
  197.4 1.2 bitcast_add_fusion.1
  198.6 1.2 bitcast_add_fusion.2
  199.9 1.0 copy-done.47
  201.6 1.1 convert_add_fusion.3
  204.7 1.5 convert_add_fusion.2
  206.9 1.0 convert_add_fusion.4
  208.1 1.3 collective-permute-start.26
  209.4 1.1 collective-permute-start.27
  210.6 7.6 %collective-permute-done.33 = bf16[2,192,768]{2,1,0:T(8,128)(2,1)S(1)} collective-permute-done((bf16[2,192,768]{2,1,0:T(8,128)(2,1)S(1)}, bf16[2,192,768]{2,1,0:T(8,128)(2,1)S(1)}, u32[]{:S(2)}, u32[]{:S(2)}) %collective-permute-start.33) | collective-permute-done | bytes 589856 | tf_op jit(solution)/shard_map/ppermute | solution.py:387
  218.3 2.1 collective-permute-start.34
  220.4 4.2 %leave_kernel.1 = (f32[512,768]{1,0:T(8,128)}, f32[2,768]{1,0:T(2,128)}) custom-call(bf16[512,768]{1,0:T(8,128)(2,1)} %bitcast.256, f32[512,768]{1,0:T(8,128)} %get-tuple-element.175.gn_ref, bf16[512,768]{1,0:T(8,128)(2,1)} %copy-done.12, f32[512,768]{1,0:T(8,128)} %get-tuple-element.177.gr_ref, f32[8,768]{1,0:T(8,128)} %convert_element_type.149.vec_ref), custom_call_target="tpu_custom_call" | custom-call | bytes 1 | tf_op jit(solution)/shard_map/leave_kernel/pallas_call | solution.py:735
  225.4 1.1 bitcast_add_fusion.5
  228.0 1.7 collective-permute-start.28
  229.8 1.2 fusion.5
  231.0 1.2 collective-permute-start.29
  233.1 2.0 collective-permute-done.29
  235.1 1.6 collective-permute-start.31
  236.7 2.6 collective-permute-done.31
  239.6 1.2 collective-permute-start.37
  240.8 2.6 collective-permute-done.32
  243.4 1.0 bitcast_add_fusion.3
  245.3 1.0 bitcast_add_fusion.4
  247.1 2.9 %collective-permute-start.35 = (bf16[192,384]{1,0:T(8,128)(2,1)}, bf16[192,384]{1,0:T(8,128)(2,1)}, u32[]{:S(2)}, u32[]{:S(2)}) collective-permute-start(bf16[192,384]{1,0:T(8,128)(2,1)} %fusion.18), channel_id=1, source_target_pairs={{0,16},{8,24},{16,0},{24,8},{1,17},{9,25},{17,1},{25,9},{2,18},{10... | collective-permute-start | bytes 442376 | tf_op jit(solution)/shard_map/ppermute | solution.py:387
  250.7 1.2 reshape.234
  251.9 4.5 %collective-permute-done.37 = bf16[512,768]{1,0:T(8,128)(2,1)} collective-permute-done((bf16[512,768]{1,0:T(8,128)(2,1)}, bf16[512,768]{1,0:T(8,128)(2,1)}, u32[]{:S(2)}, u32[]{:S(2)}) %collective-permute-start.37) | collective-permute-done | bytes 786464 | tf_op jit(solution)/shard_map/ppermute | solution.py:383
  256.4 1.1 fusion
  257.5 1.1 fusion.6
  258.6 1.2 pad_maximum_fusion.2
  259.8 0.9 pad_maximum_fusion.8
  (263 shorter events, 38.8 us)
Async XLA Ops:
  7.2 107.6 %all-gather.3.cloned.1.call-start = ((), (), s32[]{:S(2)}) async-start(), calls=%async_computation | async-start | bytes 5013504 | tf_op jit(solution)/shard_map/all_gather | solution.py:908
  9.7 2.1 copy-start.27
  9.8 1.4 collective-permute-start.10
  11.4 1.4 copy-start.32
  11.7 1.9 copy-start.17
  11.7 1.9 copy-start.18
  13.2 3.4 %collective-permute-start = (bf16[80,384]{1,0:T(8,128)(2,1)S(1)}, bf16[80,384]{1,0:T(8,128)(2,1)S(1)}, u32[]{:S(2)}, u32[]{:S(2)}) collective-permute-start(bf16[80,384]{1,0:T(8,128)(2,1)S(1)} %fusion.24), channel_id=1, source_target_pairs={{0,1},{1,0},{2,3},{3,2},{4,5},{5,4},{6,7},{7,6},{8,9},{9,8},{10,11... | collective-permute-start | bytes 184328 | tf_op jit(solution)/shard_map/ppermute | solution.py:375
  13.8 2.8 %copy-start.33 = (bf16[24,768]{1,0:T(8,128)(2,1)S(1)}, bf16[24,768]{1,0:T(8,128)(2,1)}, u32[]{:S(2)}) copy-start(bf16[24,768]{1,0:T(8,128)(2,1)} %param.24) | copy-start | bytes 110596
  13.9 26.7 %collective-permute-start.4 = (bf16[2,256,768]{2,1,0:T(8,128)(2,1)S(1)}, bf16[2,256,768]{2,1,0:T(8,128)(2,1)S(1)}, u32[]{:S(2)}, u32[]{:S(2)}) collective-permute-start(bf16[2,256,768]{2,1,0:T(8,128)(2,1)S(1)} %pad_maximum_fusion.6), channel_id=1, source_target_pairs={{0,2},{2,0},{1,3},{3,1},{4,6},{6,4},{5,7},{7,5},{8,10},{10,8},{9,1... | collective-permute-start | bytes 2359304 | tf_op jit(solution)/shard_map/ppermute | solution.py:383
  16.7 8.9 %collective-permute-start.3 = (bf16[208,384]{1,0:T(8,128)(2,1)S(1)}, bf16[208,384]{1,0:T(8,128)(2,1)S(1)}, u32[]{:S(2)}, u32[]{:S(2)}) collective-permute-start(bf16[208,384]{1,0:T(8,128)(2,1)S(1)} %pad_maximum_fusion.16), channel_id=1, source_target_pairs={{0,24},{8,16},{16,8},{24,0},{1,25},{9,17},{17,9},{25,1},{2,26},{10... | collective-permute-start | bytes 479240 | tf_op jit(solution)/shard_map/ppermute | solution.py:387
  20.4 20.1 %collective-permute-start.2 = (bf16[208,384]{1,0:T(8,128)(2,1)S(1)}, bf16[208,384]{1,0:T(8,128)(2,1)S(1)}, u32[]{:S(2)}, u32[]{:S(2)}) collective-permute-start(bf16[208,384]{1,0:T(8,128)(2,1)S(1)} %pad_maximum_fusion.16), channel_id=1, source_target_pairs={{0,16},{8,24},{16,0},{24,8},{1,17},{9,25},{17,1},{25,9},{2,18},{10... | collective-permute-start | bytes 479240 | tf_op jit(solution)/shard_map/ppermute | solution.py:387
  20.4 20.1 %collective-permute-start.1 = (bf16[208,384]{1,0:T(8,128)(2,1)S(1)}, bf16[208,384]{1,0:T(8,128)(2,1)S(1)}, u32[]{:S(2)}, u32[]{:S(2)}) collective-permute-start(bf16[208,384]{1,0:T(8,128)(2,1)S(1)} %pad_maximum_fusion.16), channel_id=1, source_target_pairs={{0,8},{8,0},{16,24},{24,16},{1,9},{9,1},{17,25},{25,17},{2,10},{10... | collective-permute-start | bytes 479240 | tf_op jit(solution)/shard_map/ppermute | solution.py:387
  40.7 14.9 %collective-permute-start.6 = (bf16[2,208,384]{2,1,0:T(8,128)(2,1)S(1)}, bf16[2,208,384]{2,1,0:T(8,128)(2,1)S(1)}, u32[]{:S(2)}, u32[]{:S(2)}) collective-permute-start(bf16[2,208,384]{2,1,0:T(8,128)(2,1)S(1)} %get-tuple-element.231), channel_id=1, source_target_pairs={{0,4},{4,0},{1,5},{5,1},{2,6},{6,2},{3,7},{7,3},{8,12},{12,8},{9,1... | collective-permute-start | bytes 958472 | tf_op jit(solution)/shard_map/ppermute | solution.py:379
  42.3 13.1 %collective-permute-start.8 = (bf16[2,208,384]{2,1,0:T(8,128)(2,1)S(1)}, bf16[2,208,384]{2,1,0:T(8,128)(2,1)S(1)}, u32[]{:S(2)}, u32[]{:S(2)}) collective-permute-start(bf16[2,208,384]{2,1,0:T(8,128)(2,1)S(1)} %get-tuple-element.232), channel_id=1, source_target_pairs={{0,2},{2,0},{1,3},{3,1},{4,6},{6,4},{5,7},{7,5},{8,10},{10,8},{9,1... | collective-permute-start | bytes 958472 | tf_op jit(solution)/shard_map/ppermute | solution.py:383
  55.5 15.2 %collective-permute-start.9 = (bf16[2,2,208,384]{3,2,0,1:T(8,128)(2,1)S(1)}, bf16[2,2,208,384]{3,2,0,1:T(8,128)(2,1)S(1)}, u32[]{:S(2)}, u32[]{:S(2)}) collective-permute-start(bf16[2,2,208,384]{3,2,0,1:T(8,128)(2,1)S(1)} %pad_maximum_fusion.10), channel_id=1, source_target_pairs={{0,4},{4,0},{1,5},{5,1},{2,6},{6,2},{3,7},{7,3},{8,12},{12,8},{9,1... | collective-permute-start | bytes 1916936 | tf_op jit(solution)/shard_map/ppermute | solution.py:379
  55.7 15.3 %collective-permute-start.7 = (bf16[2,2,208,384]{3,2,1,0:T(8,128)(2,1)S(1)}, bf16[2,2,208,384]{3,2,1,0:T(8,128)(2,1)S(1)}, u32[]{:S(2)}, u32[]{:S(2)}) collective-permute-start(bf16[2,2,208,384]{3,2,1,0:T(8,128)(2,1)S(1)} %pad_maximum_fusion.9), channel_id=1, source_target_pairs={{0,2},{2,0},{1,3},{3,1},{4,6},{6,4},{5,7},{7,5},{8,10},{10,8},{9,1... | collective-permute-start | bytes 1916936 | tf_op jit(solution)/shard_map/ppermute | solution.py:383
  58.2 12.6 %copy-start.1 = (bf16[1,2,256,768]{3,2,0,1:T(8,128)(2,1)}, bf16[1,2,256,768]{3,2,0,1:T(8,128)(2,1)S(1)}, u32[]{:S(2)}) copy-start(bf16[1,2,256,768]{3,2,0,1:T(8,128)(2,1)S(1)} %get-tuple-element.212) | copy-start | bytes 2359300
  58.2 16.6 %collective-permute-start.5 = (bf16[512,768]{1,0:T(8,128)(2,1)S(1)}, bf16[512,768]{1,0:T(8,128)(2,1)S(1)}, u32[]{:S(2)}, u32[]{:S(2)}) collective-permute-start(bf16[512,768]{1,0:T(8,128)(2,1)S(1)} %bitcast.253), channel_id=1, source_target_pairs={{0,1},{1,0},{2,3},{3,2},{4,5},{5,4},{6,7},{7,6},{8,9},{9,8},{10,11... | collective-permute-start | bytes 2359304 | tf_op jit(solution)/shard_map/ppermute | solution.py:375
  71.4 1.5 copy-start
  73.0 30.1 %collective-permute-start.11 = (bf16[8,24,768]{2,1,0:T(8,128)(2,1)S(1)}, bf16[8,24,768]{2,1,0:T(8,128)(2,1)S(1)}, u32[]{:S(2)}, u32[]{:S(2)}) collective-permute-start(bf16[8,24,768]{2,1,0:T(8,128)(2,1)S(1)} %dynamic-slice_bitcast_fusion.3), channel_id=1, source_target_pairs={{0,1},{1,0},{2,3},{3,2},{4,5},{5,4},{6,7},{7,6},{8,9},{9,8},{10,11... | collective-permute-start | bytes 884744 | tf_op jit(solution)/shard_map/ppermute | solution.py:375
  73.2 8.9 %copy-start.21 = (f32[32,8,24]{2,1,0:T(8,128)}, f32[32,8,24]{2,1,0:T(8,128)S(1)}, u32[]{:S(2)}) copy-start(f32[32,8,24]{2,1,0:T(8,128)S(1)} %reshape.240) | copy-start | bytes 73732
  103.3 5.0 %copy-start.4 = (bf16[1,2,256,768]{3,2,0,1:T(8,128)(2,1)S(1)}, bf16[1,2,256,768]{3,2,0,1:T(8,128)(2,1)}, u32[]{:S(2)}) copy-start(bf16[1,2,256,768]{3,2,0,1:T(8,128)(2,1)} %get-tuple-element.211) | copy-start | bytes 2359300
  107.7 3.1 %collective-permute-start.12 = (bf16[512,768]{1,0:T(8,128)(2,1)}, bf16[512,768]{1,0:T(8,128)(2,1)S(1)}, u32[]{:S(2)}, u32[]{:S(2)}) collective-permute-start(bf16[512,768]{1,0:T(8,128)(2,1)} %get-tuple-element.127), channel_id=1, source_target_pairs={{0,1},{1,0},{2,3},{3,2},{4,5},{5,4},{6,7},{7,6},{8,9},{9,8},{10,11... | collective-permute-start | bytes 2359304 | tf_op jit(solution)/shard_map/ppermute | solution.py:375
  108.2 7.7 %collective-permute-start.14 = (bf16[512,768]{1,0:T(8,128)(2,1)S(1)}, bf16[512,768]{1,0:T(8,128)(2,1)S(1)}, u32[]{:S(2)}, u32[]{:S(2)}) collective-permute-start(bf16[512,768]{1,0:T(8,128)(2,1)S(1)} %bitcast.263), channel_id=1, source_target_pairs={{0,1},{1,0},{2,3},{3,2},{4,5},{5,4},{6,7},{7,6},{8,9},{9,8},{10,11... | collective-permute-start | bytes 2359304 | tf_op jit(solution)/shard_map/ppermute | solution.py:375
  114.8 2.5 collective-permute-start.13
  140.5 3.0 %collective-permute-start.17 = (bf16[512,768]{1,0:T(8,128)(2,1)}, bf16[512,768]{1,0:T(8,128)(2,1)S(1)}, u32[]{:S(2)}, u32[]{:S(2)}) collective-permute-start(bf16[512,768]{1,0:T(8,128)(2,1)} %get-tuple-element.136), channel_id=1, source_target_pairs={{0,1},{1,0},{2,3},{3,2},{4,5},{5,4},{6,7},{7,6},{8,9},{9,8},{10,11... | collective-permute-start | bytes 2359304 | tf_op jit(solution)/shard_map/ppermute | solution.py:375
  141.0 29.6 %collective-permute-start.15 = (bf16[8,48,1536]{2,1,0:T(8,128)(2,1)}, bf16[8,48,1536]{2,1,0:T(8,128)(2,1)S(1)}, u32[]{:S(2)}, u32[]{:S(2)}) collective-permute-start(bf16[8,48,1536]{2,1,0:T(8,128)(2,1)} %get-tuple-element.132), channel_id=1, source_target_pairs={{0,2},{2,0},{1,3},{3,1},{4,6},{6,4},{5,7},{7,5},{8,10},{10,8},{9,1... | collective-permute-start | bytes 3538952 | tf_op jit(solution)/shard_map/ppermute | solution.py:383
  142.0 28.5 %collective-permute-start.16 = (bf16[4,2,96,768]{3,2,1,0:T(8,128)(2,1)}, bf16[4,2,96,768]{3,2,1,0:T(8,128)(2,1)S(1)}, u32[]{:S(2)}, u32[]{:S(2)}) collective-permute-start(bf16[4,2,96,768]{3,2,1,0:T(8,128)(2,1)} %get-tuple-element.133), channel_id=1, source_target_pairs={{0,4},{4,0},{1,5},{5,1},{2,6},{6,2},{3,7},{7,3},{8,12},{12,8},{9,1... | collective-permute-start | bytes 3538952 | tf_op jit(solution)/shard_map/ppermute | solution.py:379
  148.7 2.5 collective-permute-start.18
  157.5 19.4 %collective-permute-start.23 = (bf16[8,24,768]{2,1,0:T(8,128)(2,1)S(1)}, bf16[8,24,768]{2,1,0:T(8,128)(2,1)S(1)}, u32[]{:S(2)}, u32[]{:S(2)}) collective-permute-start(bf16[8,24,768]{2,1,0:T(8,128)(2,1)S(1)} %dynamic-slice_bitcast_fusion.2), channel_id=1, source_target_pairs={{0,1},{1,0},{2,3},{3,2},{4,5},{5,4},{6,7},{7,6},{8,9},{9,8},{10,11... | collective-permute-start | bytes 884744 | tf_op jit(solution)/shard_map/ppermute | solution.py:375
  157.7 13.9 %copy-start.8 = (bf16[8,48,1536]{2,1,0:T(8,128)(2,1)S(1)}, bf16[8,48,1536]{2,1,0:T(8,128)(2,1)}, u32[]{:S(2)}) copy-start(bf16[8,48,1536]{2,1,0:T(8,128)(2,1)} %get-tuple-element.131) | copy-start | bytes 3538948
  171.6 1.6 copy-start.10
  173.5 3.4 %copy-start.2 = (f32[4,2,96,768]{3,2,1,0:T(8,128)}, f32[4,2,96,768]{3,2,1,0:T(8,128)S(1)}, u32[]{:S(2)}) copy-start(f32[4,2,96,768]{3,2,1,0:T(8,128)S(1)} %convert_add_fusion) | copy-start | bytes 7077892
  173.5 3.4 %copy-start.23 = (bf16[384,768]{1,0:T(8,128)(2,1)S(1)}, bf16[384,768]{1,0:T(8,128)(2,1)}, u32[]{:S(2)}) copy-start(bf16[384,768]{1,0:T(8,128)(2,1)} %get-tuple-element.161) | copy-start | bytes 1769476
  174.5 22.8 %collective-permute-start.21 = (bf16[4,48,1536]{2,1,0:T(8,128)(2,1)}, bf16[4,48,1536]{2,1,0:T(8,128)(2,1)}, u32[]{:S(2)}, u32[]{:S(2)}) collective-permute-start(bf16[4,48,1536]{2,1,0:T(8,128)(2,1)} %fusion.3), channel_id=1, source_target_pairs={{0,4},{4,0},{1,5},{5,1},{2,6},{6,2},{3,7},{7,3},{8,12},{12,8},{9,1... | collective-permute-start | bytes 1769480 | tf_op jit(solution)/shard_map/ppermute | solution.py:379
  175.8 21.6 %collective-permute-start.22 = (bf16[4,96,768]{2,1,0:T(8,128)(2,1)S(1)}, bf16[4,96,768]{2,1,0:T(8,128)(2,1)}, u32[]{:S(2)}, u32[]{:S(2)}) collective-permute-start(bf16[4,96,768]{2,1,0:T(8,128)(2,1)S(1)} %fusion.2), channel_id=1, source_target_pairs={{0,2},{2,0},{1,3},{3,1},{4,6},{6,4},{5,7},{7,5},{8,10},{10,8},{9,1... | collective-permute-start | bytes 1769480 | tf_op jit(solution)/shard_map/ppermute | solution.py:383
  177.8 19.6 %collective-permute-start.24 = (bf16[4,2,24,768]{3,2,1,0:T(8,128)(2,1)}, bf16[4,2,24,768]{3,2,1,0:T(8,128)(2,1)}, u32[]{:S(2)}, u32[]{:S(2)}) collective-permute-start(bf16[4,2,24,768]{3,2,1,0:T(8,128)(2,1)} %dynamic-slice_bitcast_fusion.1), channel_id=1, source_target_pairs={{0,4},{4,0},{1,5},{5,1},{2,6},{6,2},{3,7},{7,3},{8,12},{12,8},{9,1... | collective-permute-start | bytes 884744 | tf_op jit(solution)/shard_map/ppermute | solution.py:379
  186.3 11.0 %copy-start.3 = (f32[4,2,96,768]{3,2,1,0:T(8,128)S(1)}, f32[4,2,96,768]{3,2,1,0:T(8,128)}, u32[]{:S(2)}) copy-start(f32[4,2,96,768]{3,2,1,0:T(8,128)} %copy-done.2) | copy-start | bytes 7077892
  186.3 18.3 %collective-permute-start.20 = (bf16[4,2,48,384]{3,2,1,0:T(8,128)(2,1)}, bf16[4,2,48,384]{3,2,1,0:T(8,128)(2,1)}, u32[]{:S(2)}, u32[]{:S(2)}) collective-permute-start(bf16[4,2,48,384]{3,2,1,0:T(8,128)(2,1)} %get-tuple-element.158), channel_id=1, source_target_pairs={{0,4},{4,0},{1,5},{5,1},{2,6},{6,2},{3,7},{7,3},{8,12},{12,8},{9,1... | collective-permute-start | bytes 884744 | tf_op jit(solution)/shard_map/ppermute | solution.py:379
  187.7 16.9 %collective-permute-start.19 = (bf16[8,96,384]{2,1,0:T(8,128)(2,1)}, bf16[8,96,384]{2,1,0:T(8,128)(2,1)}, u32[]{:S(2)}, u32[]{:S(2)}) collective-permute-start(bf16[8,96,384]{2,1,0:T(8,128)(2,1)} %get-tuple-element.157), channel_id=1, source_target_pairs={{0,2},{2,0},{1,3},{3,1},{4,6},{6,4},{5,7},{7,5},{8,10},{10,8},{9,1... | collective-permute-start | bytes 1769480 | tf_op jit(solution)/shard_map/ppermute | solution.py:383
  197.3 5.9 %collective-permute-start.30 = (bf16[512,768]{1,0:T(8,128)(2,1)}, bf16[512,768]{1,0:T(8,128)(2,1)S(1)}, u32[]{:S(2)}, u32[]{:S(2)}) collective-permute-start(bf16[512,768]{1,0:T(8,128)(2,1)} %get-tuple-element.188), channel_id=1, source_target_pairs={{0,1},{1,0},{2,3},{3,2},{4,5},{5,4},{6,7},{7,6},{8,9},{9,8},{10,11... | collective-permute-start | bytes 2359304 | tf_op jit(solution)/shard_map/ppermute | solution.py:375
  200.9 3.8 %collective-permute-start.25 = (bf16[512,768]{1,0:T(8,128)(2,1)S(1)}, bf16[512,768]{1,0:T(8,128)(2,1)S(1)}, u32[]{:S(2)}, u32[]{:S(2)}) collective-permute-start(bf16[512,768]{1,0:T(8,128)(2,1)S(1)} %copy-done.47), channel_id=1, source_target_pairs={{0,1},{1,0},{2,3},{3,2},{4,5},{5,4},{6,7},{7,6},{8,9},{9,8},{10,11... | collective-permute-start | bytes 2359304 | tf_op jit(solution)/shard_map/ppermute | solution.py:375
  201.6 1.7 copy-start.6
  202.7 1.5 copy-start.5
  202.7 1.5 copy-start.34
  202.8 15.3 %collective-permute-start.33 = (bf16[2,192,768]{2,1,0:T(8,128)(2,1)S(1)}, bf16[2,192,768]{2,1,0:T(8,128)(2,1)S(1)}, u32[]{:S(2)}, u32[]{:S(2)}) collective-permute-start(bf16[2,192,768]{2,1,0:T(8,128)(2,1)S(1)} %fusion.4), channel_id=1, source_target_pairs={{0,8},{8,0},{16,24},{24,16},{1,9},{9,1},{17,25},{25,17},{2,10},{10... | collective-permute-start | bytes 1769480 | tf_op jit(solution)/shard_map/ppermute | solution.py:387
  203.3 1.4 copy-start.22
  204.7 2.3 copy-start.12
  204.7 2.3 copy-start.24
  208.1 16.6 %collective-permute-start.26 = (bf16[4,96,384]{2,1,0:T(8,128)(2,1)}, bf16[4,96,384]{2,1,0:T(8,128)(2,1)S(1)}, u32[]{:S(2)}, u32[]{:S(2)}) collective-permute-start(bf16[4,96,384]{2,1,0:T(8,128)(2,1)} %fusion.12), channel_id=1, source_target_pairs={{0,4},{4,0},{1,5},{5,1},{2,6},{6,2},{3,7},{7,3},{8,12},{12,8},{9,1... | collective-permute-start | bytes 884744 | tf_op jit(solution)/shard_map/ppermute | solution.py:379
  209.4 15.2 %collective-permute-start.27 = (bf16[4,96,384]{2,1,0:T(8,128)(2,1)S(1)}, bf16[4,96,384]{2,1,0:T(8,128)(2,1)}, u32[]{:S(2)}, u32[]{:S(2)}) collective-permute-start(bf16[4,96,384]{2,1,0:T(8,128)(2,1)S(1)} %fusion.10), channel_id=1, source_target_pairs={{0,2},{2,0},{1,3},{3,1},{4,6},{6,4},{5,7},{7,5},{8,10},{10,8},{9,1... | collective-permute-start | bytes 884744 | tf_op jit(solution)/shard_map/ppermute | solution.py:383
  218.3 22.5 %collective-permute-start.34 = (bf16[192,768]{1,0:T(8,128)(2,1)S(1)}, bf16[192,768]{1,0:T(8,128)(2,1)}, u32[]{:S(2)}, u32[]{:S(2)}) collective-permute-start(bf16[192,768]{1,0:T(8,128)(2,1)S(1)} %fusion.11), channel_id=1, source_target_pairs={{0,16},{8,24},{16,0},{24,8},{1,17},{9,25},{17,1},{25,9},{2,18},{10... | collective-permute-start | bytes 884744 | tf_op jit(solution)/shard_map/ppermute | solution.py:387
  228.0 15.4 %collective-permute-start.28 = (bf16[2,192,384]{2,1,0:T(8,128)(2,1)}, bf16[2,192,384]{2,1,0:T(8,128)(2,1)}, u32[]{:S(2)}, u32[]{:S(2)}) collective-permute-start(bf16[2,192,384]{2,1,0:T(8,128)(2,1)} %fusion.13), channel_id=1, source_target_pairs={{0,8},{8,0},{16,24},{24,16},{1,9},{9,1},{17,25},{25,17},{2,10},{10... | collective-permute-start | bytes 884744 | tf_op jit(solution)/shard_map/ppermute | solution.py:387
  231.0 4.2 %collective-permute-start.29 = (f32[10,768]{1,0:T(8,128)S(1)}, f32[10,768]{1,0:T(8,128)S(1)}, u32[]{:S(2)}, u32[]{:S(2)}) collective-permute-start(f32[10,768]{1,0:T(8,128)S(1)} %pad_maximum_fusion.22), channel_id=1, source_target_pairs={{0,2},{2,0},{1,3},{3,1},{4,6},{6,4},{5,7},{7,5},{8,10},{10,8},{9,1... | collective-permute-start | bytes 92168 | tf_op jit(solution)/shard_map/ppermute | solution.py:383
  235.1 4.2 %collective-permute-start.31 = (f32[10,768]{1,0:T(8,128)S(1)}, f32[10,768]{1,0:T(8,128)S(1)}, u32[]{:S(2)}, u32[]{:S(2)}) collective-permute-start(f32[10,768]{1,0:T(8,128)S(1)} %add.187), channel_id=1, source_target_pairs={{0,4},{4,0},{1,5},{5,1},{2,6},{6,2},{3,7},{7,3},{8,12},{12,8},{9,1... | collective-permute-start | bytes 92168 | tf_op jit(solution)/shard_map/ppermute | solution.py:379
  239.3 4.2 %collective-permute-start.32 = (f32[10,768]{1,0:T(8,128)S(1)}, f32[10,768]{1,0:T(8,128)S(1)}, u32[]{:S(2)}, u32[]{:S(2)}) collective-permute-start(f32[10,768]{1,0:T(8,128)S(1)} %add.193), channel_id=1, source_target_pairs={{0,8},{8,0},{16,24},{24,16},{1,9},{9,1},{17,25},{25,17},{2,10},{10... | collective-permute-start | bytes 92168 | tf_op jit(solution)/shard_map/ppermute | solution.py:387
  239.6 16.8 %collective-permute-start.37 = (bf16[512,768]{1,0:T(8,128)(2,1)}, bf16[512,768]{1,0:T(8,128)(2,1)}, u32[]{:S(2)}, u32[]{:S(2)}) collective-permute-start(bf16[512,768]{1,0:T(8,128)(2,1)} %pad_maximum_fusion.7), channel_id=1, source_target_pairs={{0,2},{2,0},{1,3},{3,1},{4,6},{6,4},{5,7},{7,5},{8,10},{10,8},{9,1... | collective-permute-start | bytes 2359304 | tf_op jit(solution)/shard_map/ppermute | solution.py:383
  243.4 1.8 copy-start.28
  245.2 4.8 %collective-permute-start.38 = (f32[2,24,768]{2,1,0:T(8,128)S(1)}, f32[2,24,768]{2,1,0:T(8,128)S(1)}, u32[]{:S(2)}, u32[]{:S(2)}) collective-permute-start(f32[2,24,768]{2,1,0:T(8,128)S(1)} %dynamic-slice_bitcast_fusion.4), channel_id=1, source_target_pairs={{0,1},{1,0},{2,3},{3,2},{4,5},{5,4},{6,7},{7,6},{8,9},{9,8},{10,11... | collective-permute-start | bytes 442376 | tf_op jit(solution)/shard_map/ppermute | solution.py:375
  246.4 14.4 %collective-permute-start.36 = (f32[10,768]{1,0:T(8,128)S(1)}, f32[10,768]{1,0:T(8,128)}, u32[]{:S(2)}, u32[]{:S(2)}) collective-permute-start(f32[10,768]{1,0:T(8,128)S(1)} %add.199), channel_id=1, source_target_pairs={{0,16},{8,24},{16,0},{24,8},{1,17},{9,25},{17,1},{25,9},{2,18},{10... | collective-permute-start | bytes 92168 | tf_op jit(solution)/shard_map/ppermute | solution.py:387
  247.1 13.6 %collective-permute-start.35 = (bf16[192,384]{1,0:T(8,128)(2,1)}, bf16[192,384]{1,0:T(8,128)(2,1)}, u32[]{:S(2)}, u32[]{:S(2)}) collective-permute-start(bf16[192,384]{1,0:T(8,128)(2,1)} %fusion.18), channel_id=1, source_target_pairs={{0,16},{8,24},{16,0},{24,8},{1,17},{9,25},{17,1},{25,9},{2,18},{10... | collective-permute-start | bytes 442376 | tf_op jit(solution)/shard_map/ppermute | solution.py:387
  250.2 6.2 %copy-start.11 = (f32[512,768]{1,0:T(8,128)S(1)}, f32[512,768]{1,0:T(8,128)}, u32[]{:S(2)}) copy-start(f32[512,768]{1,0:T(8,128)} %get-tuple-element.189) | copy-start | bytes 4718596
  262.6 1.9 collective-permute-start.40
  262.7 2.4 collective-permute-start.39
  (26 other events, 28.2 us)
Sparse Core Ops, SparseCore 0:
  12.7 92.1 all-gather.2
